TPU v7x, 128 devices: a whole 4x4x4 slice. The times are simulated.
128 devices in a mesh: prompt: 4 (over x), sample: 32 (over z, y, core).
Axes of the slice: x: 4, y: 4, z: 4, core: 2. Of those that a mesh axis runs over, the one named last changes fastest.
Arguments:
- prompt_cache: bfloat16 [4, 4096, 1024], P('prompt', 'sample'), may hold values from -6 to 6
- queries: bfloat16 [2, 2048, 8192], P(None, ('prompt', 'sample')), may hold values from -140 to 140
- new_kv: bfloat16 [2, 2048, 1024], P(None, ('prompt', 'sample')), may hold values from -12 to 12
- residual: bfloat16 [2, 2048, 4096], P(None, ('prompt', 'sample')), may hold values from -6 to 6
- out_weight: bfloat16 [8192, 4096], P('sample'), may hold values from -0.25 to 0.25
- norm_gain: float32 [4096], replicated, may hold values from 0.1 to 1.9
- gate_up: bfloat16 [128, 4096, 1536], P(('prompt', 'sample')), may hold values from -0.09375 to 0.09375
- down_weight: bfloat16 [128, 768, 4096], P(('prompt', 'sample')), may hold values from -0.21875 to 0.21875
- expert_ids: int32 [2, 2048, 8], P(None, ('prompt', 'sample')), may hold values from 0 to 127, all different within a row; in each aligned block of 16 rows (0 to 15, 16 to 31, ..., all dimensions but the last counted through in order) at most 2 rows name the same one
- route_weights: float32 [2, 2048, 8], P(None, ('prompt', 'sample')), may hold values from 0.1 to 1
Outputs:
- layer_out: bfloat16 [2, 2048, 4096], P(None, ('prompt', 'sample'))
Inputs may be any that keep to these rules, and one draw needn't show every extreme that they name: `expert_ids`: each row names 8 different experts. Within the 16 rows of one device in one step (aligned blocks along the rows of a step) no expert is named by more than 2 rows, a bound that some block reaches.
All inputs are finite; a program needn't handle non-finite values.
Results may differ from a plain program's by a relative error of at most 0.022.
Values may be sent and summed in bfloat16 or wider, within the bound.
No kernel may reach another device: no remote copies, remote signals or barrier semaphores. Data moves between devices by JAX's collectives and lax.ppermute only.
A program may use at most 128 MiB of HBM per device.

v0:
```python
import jax
import jax.numpy as jnp
from jax import lax
from jax.sharding import PartitionSpec as P

QH = 64
KVH = 4
HD = 128


EPSILON = 1e-06
NEG_LARGE = -1e30


def online_update(state_in, grouped, key_block, value_block, score_scale):
    running, row_total, accumulated = state_in
    scores = (
        jnp.einsum("kmd,nkd->kmn", grouped, key_block, preferred_element_type=jnp.float32)
        * score_scale
    )
    largest = jnp.maximum(running, jnp.max(scores, axis=-1))
    factor = jnp.exp(running - largest)
    weights = jnp.exp(scores - largest[..., None])
    row_total = row_total * factor + jnp.sum(weights, axis=-1)
    accumulated = accumulated * factor[..., None] + jnp.einsum(
        "kmn,nkd->kmd",
        weights.astype(jnp.bfloat16),
        value_block,
        preferred_element_type=jnp.float32,
    )
    return (largest, row_total, accumulated)


def attend(prompt_cache, query_rows, new_kv, first_step, score_scale):
    step_count, row_count = (query_rows.shape[0], query_rows.shape[1])
    group_size = QH // KVH
    merged = step_count * row_count * group_size
    grouped = (
        query_rows.reshape(step_count, row_count, KVH, group_size, HD)
        .transpose(2, 0, 1, 3, 4)
        .reshape(KVH, merged, HD)
    )
    initial = (
        jnp.full((KVH, merged), NEG_LARGE, jnp.float32),
        jnp.zeros((KVH, merged), jnp.float32),
        jnp.zeros((KVH, merged, HD), jnp.float32),
    )
    piece = lax.all_gather(prompt_cache, "sample", axis=1, tiled=True)
    length = piece.shape[1]
    block_len = 1024
    blocks = piece.reshape(length // block_len, block_len, 2, KVH, HD)

    def one_block(state_now, block_data):
        return (
            online_update(state_now, grouped, block_data[:, 0], block_data[:, 1], score_scale),
            None,
        )

    state_out, unused = lax.scan(one_block, initial, blocks)
    running, row_total, accumulated = state_out
    steps_all = new_kv.shape[0]
    fresh_kv = new_kv.reshape(steps_all, row_count, 2, KVH, HD)
    shaped = grouped.reshape(KVH, step_count, row_count, group_size, HD)
    fresh_scores = (
        jnp.einsum(
            "ksrgd,trkd->ksrgt", shaped, fresh_kv[:, :, 0], preferred_element_type=jnp.float32
        )
        * score_scale
    )
    visible = (jnp.arange(steps_all)[None, :] <= (first_step + jnp.arange(step_count))[:, None])[
        None, :, None, None, :
    ]
    fresh_scores = jnp.where(visible, fresh_scores, NEG_LARGE)
    running = running.reshape(KVH, step_count, row_count, group_size)
    largest = jnp.maximum(running, jnp.max(fresh_scores, axis=-1))
    factor = jnp.exp(running - largest)
    fresh_weights = jnp.where(visible, jnp.exp(fresh_scores - largest[..., None]), 0.0)
    row_total = row_total.reshape(KVH, step_count, row_count, group_size) * factor + jnp.sum(
        fresh_weights, axis=-1
    )
    accumulated = (
        accumulated.reshape(KVH, step_count, row_count, group_size, HD) * factor[..., None]
    )
    accumulated = accumulated + jnp.einsum(
        "ksrgt,trkd->ksrgd",
        fresh_weights.astype(jnp.bfloat16),
        fresh_kv[:, :, 1],
        preferred_element_type=jnp.float32,
    )
    output = (accumulated / row_total[..., None]).astype(jnp.bfloat16)
    return output.transpose(1, 2, 0, 3, 4).reshape(step_count, row_count, QH * HD)


def project(attended, out_weight):
    step_count, row_count, width_all = attended.shape
    row_major = attended.transpose(1, 0, 2).reshape(row_count * step_count, width_all)
    spread = lax.all_to_all(row_major, "sample", split_axis=1, concat_axis=0, tiled=True)
    summed = lax.psum_scatter(
        jnp.dot(spread, out_weight, preferred_element_type=jnp.float32).astype(jnp.bfloat16),
        "sample",
        scatter_dimension=0,
        tiled=True,
    ).astype(jnp.float32)
    return summed.reshape(row_count, step_count, -1).transpose(1, 0, 2)


def slot_numbers(expert_ids, experts, capacity):
    step_count, row_count, top_count = expert_ids.shape
    onehot = (expert_ids[..., None] == jnp.arange(experts, dtype=jnp.int32)).astype(jnp.int32)
    blocked = onehot.reshape(step_count, row_count * top_count, experts)
    ranked = jnp.sum((jnp.cumsum(blocked, axis=1) - blocked) * blocked, axis=-1).reshape(
        step_count, row_count, top_count
    )
    return (
        expert_ids * (step_count * capacity)
        + jnp.arange(step_count, dtype=jnp.int32)[:, None, None] * capacity
        + ranked
    )


def expert_apply(arrived, gate_up, down_weight):
    projected = jnp.einsum("scd,df->scf", arrived, gate_up, preferred_element_type=jnp.float32)
    middle = projected.shape[-1] // 2
    active = (jax.nn.silu(projected[..., :middle]) * projected[..., middle:]).astype(jnp.bfloat16)
    return jnp.einsum(
        "scf,fd->scd", active, down_weight, preferred_element_type=jnp.float32
    ).astype(jnp.bfloat16)


def run_experts(outgoing, gate_up, down_weight):
    return lax.all_to_all(
        expert_apply(
            lax.all_to_all(outgoing, ("prompt", "sample"), split_axis=0, concat_axis=0, tiled=True),
            gate_up,
            down_weight,
        ),
        ("prompt", "sample"),
        split_axis=0,
        concat_axis=0,
        tiled=True,
    )


def on_device(
    prompt_cache,
    queries,
    new_kv,
    residual,
    out_weight,
    norm_gain,
    gate_up,
    down_weight,
    expert_ids,
    route_weights,
):
    steps_all, row_count, top_count = expert_ids.shape
    prompt_size = lax.axis_size("prompt")
    sample_size = lax.axis_size("sample")
    experts = prompt_size * sample_size * gate_up.shape[0]
    capacity = max(2, 2 * row_count * top_count // experts)
    score_scale = HD ** (-0.5)
    step_spans = [(step_index, 1) for step_index in range(steps_all)]
    results = []
    for first_step, step_count in step_spans:
        end_step = first_step + step_count
        attended = attend(
            prompt_cache, queries[first_step:end_step], new_kv, first_step, score_scale
        )
        hidden = residual[first_step:end_step].astype(jnp.float32) + project(attended, out_weight)
        moment = jnp.mean(hidden * hidden, axis=-1, keepdims=True)
        normed = (hidden * lax.rsqrt(moment + EPSILON) * norm_gain).astype(jnp.bfloat16)
        slot_ids = slot_numbers(expert_ids[first_step:end_step], experts, capacity)
        positions = jnp.arange(experts * step_count * capacity, dtype=jnp.int32)
        per_row = slot_ids.reshape(step_count * row_count, top_count)
        dispatch_map = jnp.any(per_row[None, :, :] == positions[:, None, None], axis=-1).astype(
            jnp.bfloat16
        )
        outgoing = jnp.dot(
            dispatch_map,
            normed.reshape(step_count * row_count, -1),
            preferred_element_type=jnp.float32,
        ).astype(jnp.bfloat16)
        outgoing = outgoing.reshape(experts, step_count * capacity, -1)
        returned = run_experts(outgoing, gate_up[0], down_weight[0])
        pick_map = (per_row.reshape(-1)[:, None] == positions[None, :]).astype(jnp.bfloat16)
        gathered = jnp.dot(
            pick_map,
            returned.reshape(experts * step_count * capacity, -1),
            preferred_element_type=jnp.float32,
        )
        chosen_weights = route_weights[first_step:end_step].reshape(
            step_count * row_count, top_count, 1
        )
        mixture = jnp.sum(
            gathered.reshape(step_count * row_count, top_count, -1) * chosen_weights, axis=1
        )
        results.append((hidden + mixture.reshape(step_count, row_count, -1)).astype(jnp.bfloat16))
    return jnp.concatenate(results, axis=0)


def solution(mesh):
    in_specs = (
        P("prompt", "sample", None),
        P(None, ("prompt", "sample"), None),
        P(None, ("prompt", "sample"), None),
        P(None, ("prompt", "sample"), None),
        P("sample", None),
        P(),
        P(("prompt", "sample"), None, None),
        P(("prompt", "sample"), None, None),
        P(None, ("prompt", "sample"), None),
        P(None, ("prompt", "sample"), None),
    )
    out_specs = P(None, ("prompt", "sample"), None)
    return jax.shard_map(
        on_device, mesh=mesh, in_specs=in_specs, out_specs=out_specs, check_vma=False
    )
```

profile of v0, /device:TPU:1, one launch (start us, length us, event | category | flops | bytes accessed | tf_op | source)
XLA Modules:
  0.0 479.6 jit_solution(6552577899350184629)
XLA Ops:
  13.2 53.1 %all-gather.2.cloned.1.call-done = bf16[1,4096,1024]{2,1,0:T(8,128)(2,1)} async-done(((bf16[1,128,1024]{2,1,0:T(8,128)(2,1)}), bf16[1,4096,1024]{2,1,0:T(8,128)(2,1)}) %all-gather.2.cloned.1.call-update) | async-done | bytes 8388624 | tf_op jit(solution)/shard_map/all_gather | solution.py:48
  66.3 14.3 %reshape.551 = bf16[4,1024,2,4,128]{4,3,2,1,0:T(4,128)(2,1)} reshape(bf16[1,4096,1024]{2,1,0:T(8,128)(2,1)} %all-gather.2.cloned.1.call-done) | data formatting | bytes 16777216 | tf_op jit(solution)/shard_map/reshape | solution.py:51
  80.7 8.7 %copy.80 = bf16[4,1024,2,4,128]{4,1,3,2,0:T(8,128)(2,1)} copy(bf16[4,1024,2,4,128]{4,3,2,1,0:T(4,128)(2,1)} %reshape.551) | data formatting | bytes 16777216
  89.4 17.7 %while.30 = (s32[]{:T(128)}, f32[4,256]{1,0:T(4,128)S(1)}, f32[4,256]{1,0:T(4,128)S(1)}, f32[4,256,128]{2,1,0:T(8,128)S(1)}, bf16[4,1024,2,4,128]{4,1,3,2,0:T(8,...) while((s32[]{:T(128)}, f32[4,256]{1,0:T(4,128)S(1)}, f32[4,256]{1,0:T(4,128)S(1)}, ...), condition=%wide.region_3.4_spmd.clone, body=%wide.region_0.3_spmd.clone.sunk | while | flops 545657856 | bytes 21299336 | solution.py:59
  107.3 17.5 %while.31 = (s32[]{:T(128)}, f32[4,256]{1,0:T(4,128)S(1)}, f32[4,256]{1,0:T(4,128)S(1)}, f32[4,256,128]{2,1,0:T(8,128)S(1)}, bf16[4,1024,2,4,128]{4,1,3,2,0:T(8,...) while((s32[]{:T(128)}, f32[4,256]{1,0:T(4,128)S(1)}, ...), condition=%wide.region_15.16_spmd.clone, body=%wide.region_12.15_spmd.clone.sunk | while | flops 545657856 | bytes 20250732 | solution.py:59
  129.2 14.2 %all_to_all.58 = bf16[16,32,256]{2,0,1:T(8,128)(2,1)S(1)} all-to-all(bf16[16,32,256]{2,0,1:T(8,128)(2,1)S(1)} %copy.84), channel_id=1, replica_groups=mesh['prompt'=4,'sample'=32] {'sample'}, dimensions={1} | all-to-all | bytes 524288 | tf_op jit(solution)/shard_map/all_to_all | solution.py:97
  148.2 12.5 %all_to_all.59 = bf16[16,32,256]{2,0,1:T(8,128)(2,1)S(1)} all-to-all(bf16[16,32,256]{2,0,1:T(8,128)(2,1)S(1)} %copy.95), channel_id=1, replica_groups=mesh['prompt'=4,'sample'=32] {'sample'}, dimensions={1} | all-to-all | bytes 524288 | tf_op jit(solution)/shard_map/all_to_all | solution.py:97
  165.4 59.2 %reduce-scatter.3.cloned.1.call-done = bf16[16,4096]{1,0:T(8,128)(2,1)} async-done(((bf16[512,4096]{1,0:T(8,128)(2,1)}), bf16[16,4096]{1,0:T(8,128)(2,1)}) %reduce-scatter.3.cloned.1.call-update) | async-done | bytes 131088 | tf_op jit(solution)/shard_map/reduce_scatter | solution.py:98
  224.6 85.4 %reduce-scatter.5.cloned.1.call-done = bf16[16,4096]{1,0:T(8,128)(2,1)} async-done(((bf16[512,4096]{1,0:T(8,128)(2,1)}), bf16[16,4096]{1,0:T(8,128)(2,1)}) %reduce-scatter.5.cloned.1.call-update) | async-done | bytes 131088 | tf_op jit(solution)/shard_map/reduce_scatter | solution.py:98
  314.2 4.4 reshape.574
  318.6 9.5 %all-to-all-start.4 = ((bf16[128,2,4096]{2,1,0:T(2,128)(2,1)}), bf16[128,2,4096]{2,1,0:T(2,128)(2,1)}, u32[]{:S(2)}, u32[]{:S(2)}) async-start(bf16[128,2,4096]{2,1,0:T(2,128)(2,1)} %reshape.574), calls=%async_computation.6 | async-start | bytes 4194304 | tf_op jit(solution)/shard_map/all_to_all | solution.py:133
  331.1 4.4 reshape.562
  335.5 22.7 %all-to-all-done.4 = bf16[128,2,4096]{2,1,0:T(2,128)(2,1)} async-done(((bf16[128,2,4096]{2,1,0:T(2,128)(2,1)}), bf16[128,2,4096]{2,1,0:T(2,128)(2,1)}, u32[]{:S(2)}, u32[]{:S(2)}) %all-to-all-start.4) | async-done | bytes 2097184 | tf_op jit(solution)/shard_map/all_to_all | solution.py:133
  358.2 5.6 %all-to-all-start.1 = ((bf16[128,2,4096]{2,1,0:T(2,128)(2,1)}), bf16[128,2,4096]{2,1,0:T(2,128)(2,1)}, u32[]{:S(2)}, u32[]{:S(2)}) async-start(bf16[128,2,4096]{2,1,0:T(2,128)(2,1)} %reshape.562), calls=%async_computation.2 | async-start | bytes 4194304 | tf_op jit(solution)/shard_map/all_to_all | solution.py:133
  363.8 10.7 %fusion.26 = f32[128,2,1536]{2,0,1:T(8,128)S(1)} fusion(bf16[1,4096,1536]{2,1,0:T(8,128)(2,1)} %param.20, bf16[128,2,4096]{2,1,0:T(2,128)(2,1)} %all-to-all-done.4), kind=kOutput, calls=%fused_computation.38 | convolution fusion | flops 3221225472 | bytes 16252928 | tf_op jit(solution)/shard_map/scd,df->scf/dot_general | solution.py:122
  374.5 4.6 fusion.37
  382.7 11.3 %all-to-all-done.1 = bf16[128,2,4096]{2,1,0:T(2,128)(2,1)} async-done(((bf16[128,2,4096]{2,1,0:T(2,128)(2,1)}), bf16[128,2,4096]{2,1,0:T(2,128)(2,1)}, u32[]{:S(2)}, u32[]{:S(2)}) %all-to-all-start.1) | async-done | bytes 2097184 | tf_op jit(solution)/shard_map/all_to_all | solution.py:133
  394.0 5.6 %all-to-all-start.5 = ((bf16[128,2,4096]{2,1,0:T(2,128)(2,1)}), bf16[128,2,4096]{2,1,0:T(2,128)(2,1)}, u32[]{:S(2)}, u32[]{:S(2)}) async-start(bf16[128,2,4096]{2,1,0:T(2,128)(2,1)} %copy.101), calls=%async_computation.7 | async-start | bytes 4194304 | tf_op jit(solution)/shard_map/all_to_all | solution.py:131
  399.6 10.7 %fusion.28 = f32[128,2,1536]{2,0,1:T(8,128)S(1)} fusion(bf16[1,4096,1536]{2,1,0:T(8,128)(2,1)} %param.20, bf16[128,2,4096]{2,1,0:T(2,128)(2,1)} %all-to-all-done.1), kind=kOutput, calls=%fused_computation.40 | convolution fusion | flops 3221225472 | bytes 16252928 | tf_op jit(solution)/shard_map/scd,df->scf/dot_general | solution.py:122
  410.3 4.6 fusion.34
  418.5 11.3 %all-to-all-done.5 = bf16[128,2,4096]{2,1,0:T(2,128)(2,1)} async-done(((bf16[128,2,4096]{2,1,0:T(2,128)(2,1)}), bf16[128,2,4096]{2,1,0:T(2,128)(2,1)}, u32[]{:S(2)}, u32[]{:S(2)}) %all-to-all-start.5) | async-done | bytes 2097184 | tf_op jit(solution)/shard_map/all_to_all | solution.py:131
  429.8 5.6 %all-to-all-start.2 = ((bf16[128,2,4096]{2,1,0:T(2,128)(2,1)}), bf16[128,2,4096]{2,1,0:T(2,128)(2,1)}, u32[]{:S(2)}, u32[]{:S(2)}) async-start(bf16[128,2,4096]{2,1,0:T(2,128)(2,1)} %copy.90), calls=%async_computation.3 | async-start | bytes 4194304 | tf_op jit(solution)/shard_map/all_to_all | solution.py:131
  435.6 4.1 reshape.582
  442.2 23.4 %all-to-all-done.2 = bf16[128,2,4096]{2,1,0:T(2,128)(2,1)} async-done(((bf16[128,2,4096]{2,1,0:T(2,128)(2,1)}), bf16[128,2,4096]{2,1,0:T(2,128)(2,1)}, u32[]{:S(2)}, u32[]{:S(2)}) %all-to-all-start.2) | async-done | bytes 2097184 | tf_op jit(solution)/shard_map/all_to_all | solution.py:131
  (164 shorter events, 79.6 us)
Async XLA Ops:
  6.5 136.8 %copy-start = (bf16[256,4096]{1,0:T(8,128)(2,1)S(1)}, bf16[256,4096]{1,0:T(8,128)(2,1)}, u32[]{:S(2)}) copy-start(bf16[256,4096]{1,0:T(8,128)(2,1)} %param.18) | copy-start | bytes 6291460
  6.5 59.8 %all-gather.2.cloned.1.call-start = ((), (), s32[]{:S(2)}) async-start(), calls=%async_computation.8 | async-start | bytes 8650752 | tf_op jit(solution)/shard_map/all_gather | solution.py:48
  7.3 217.3 %reduce-scatter.3.cloned.1.call-start = ((), (), s32[]{:S(2)}) async-start(), calls=%async_computation.9 | async-start | bytes 4325376 | tf_op jit(solution)/shard_map/reduce_scatter | solution.py:98
  10.2 2.1 copy-start.11
  10.2 2.1 copy-start.9
  89.4 1.8 copy-start.1
  93.8 1.8 copy-start.1
  98.2 1.8 copy-start.1
  102.7 1.8 copy-start.1
  107.3 19.1 %copy-start.10 = (pred[2]{0:T(512)(128)(4,1)S(1)}, pred[2]{0:T(512)(128)(4,1)}, u32[]{:S(2)}) copy-start(pred[2]{0:T(512)(128)(4,1)} %copy-done.9) | copy-start | bytes 10
  107.3 19.1 %copy-start.12 = (pred[2]{0:T(512)(128)(4,1)S(1)}, pred[2]{0:T(512)(128)(4,1)}, u32[]{:S(2)}) copy-start(pred[2]{0:T(512)(128)(4,1)} %copy-done.11) | copy-start | bytes 10
  146.6 0.8 copy-start.6
  146.6 163.4 %reduce-scatter.5.cloned.1.call-start = ((), (), s32[]{:S(2)}) async-start(), calls=%async_computation.10 | async-start | bytes 4325376 | tf_op jit(solution)/shard_map/reduce_scatter | solution.py:98
  163.8 0.7 copy-start.7
  163.9 146.2 %copy-start.2 = (bf16[2,16,4096]{2,1,0:T(8,128)(2,1)S(1)}, bf16[2,16,4096]{2,1,0:T(8,128)(2,1)}, u32[]{:S(2)}) copy-start(bf16[2,16,4096]{2,1,0:T(8,128)(2,1)} %param.17) | copy-start | bytes 786436
  163.9 147.3 %copy-start.5 = (f32[4096]{0:T(1024)S(1)}, f32[4096]{0:T(1024)}, u32[]{:S(2)}) copy-start(f32[4096]{0:T(1024)} %param.19) | copy-start | bytes 49156
  318.6 10.4 %copy-start.3 = (bf16[16,4096]{1,0:T(8,128)(2,1)S(1)}, bf16[16,4096]{1,0:T(8,128)(2,1)}, u32[]{:S(2)}) copy-start(bf16[16,4096]{1,0:T(8,128)(2,1)} %reduce-scatter.3.cloned.1.call-done) | copy-start | bytes 393220
  318.6 39.6 %all-to-all-start.4 = ((bf16[128,2,4096]{2,1,0:T(2,128)(2,1)}), bf16[128,2,4096]{2,1,0:T(2,128)(2,1)}, u32[]{:S(2)}, u32[]{:S(2)}) async-start(bf16[128,2,4096]{2,1,0:T(2,128)(2,1)} %reshape.574), calls=%async_computation.6 | async-start | bytes 4194304 | tf_op jit(solution)/shard_map/all_to_all | solution.py:133
  358.2 35.8 %all-to-all-start.1 = ((bf16[128,2,4096]{2,1,0:T(2,128)(2,1)}), bf16[128,2,4096]{2,1,0:T(2,128)(2,1)}, u32[]{:S(2)}, u32[]{:S(2)}) async-start(bf16[128,2,4096]{2,1,0:T(2,128)(2,1)} %reshape.562), calls=%async_computation.2 | async-start | bytes 4194304 | tf_op jit(solution)/shard_map/all_to_all | solution.py:133
  394.0 35.8 %all-to-all-start.5 = ((bf16[128,2,4096]{2,1,0:T(2,128)(2,1)}), bf16[128,2,4096]{2,1,0:T(2,128)(2,1)}, u32[]{:S(2)}, u32[]{:S(2)}) async-start(bf16[128,2,4096]{2,1,0:T(2,128)(2,1)} %copy.101), calls=%async_computation.7 | async-start | bytes 4194304 | tf_op jit(solution)/shard_map/all_to_all | solution.py:131
  418.5 16.9 %copy-start.8 = (f32[2,16,8]{1,2,0:T(8,128)S(1)}, f32[2,16,8]{1,2,0:T(8,128)}, u32[]{:S(2)}) copy-start(f32[2,16,8]{1,2,0:T(8,128)} %param.23) | copy-start | bytes 3076
  429.8 35.8 %all-to-all-start.2 = ((bf16[128,2,4096]{2,1,0:T(2,128)(2,1)}), bf16[128,2,4096]{2,1,0:T(2,128)(2,1)}, u32[]{:S(2)}, u32[]{:S(2)}) async-start(bf16[128,2,4096]{2,1,0:T(2,128)(2,1)} %copy.90), calls=%async_computation.3 | async-start | bytes 4194304 | tf_op jit(solution)/shard_map/all_to_all | solution.py:131
  469.7 2.5 copy-start.4
  472.4 0.7 copy-start.13
Sparse Core Ops, SparseCore 0:
  9.6 56.6 all-gather.1
  146.7 77.8 reduce-scatter.2
  228.7 81.2 reduce-scatter.4
where the time goes:
time: 481 us; the launch traced here: 480 us
  waiting for transfers between devices  267 us (56%)
  local copies, waits for them, and re-layouts  68.2 us (14%)
  matrix products  66.3 us (14%)
  blocking collectives  26.7 us (6%)
  starting transfers between devices  26.5 us (6%)
  between operations  13.5 us (3%)
  other arithmetic  10.9 us (2%)
    reduce_scatter x2, waiting for transfers between devices, project(): lax.psum_scatter(jnp.dot(spread, out_weight, preferred_element_type=jnp.f...  145 us
    all_gather x1, waiting for transfers between devices, attend(): piece = lax.all_gather(prompt_cache, 'sample', axis=1, tiled=True)  53.1 us
    all_to_all x2, waiting for transfers between devices, run_experts(): lax.all_to_all(expert_apply(lax.all_to_all(outgoing, ('prompt', 'sample')...  34.7 us
    all_to_all x2, waiting for transfers between devices, run_experts(): lax.all_to_all(outgoing, ('prompt', 'sample'), split_axis=0, concat_axis=...  34 us
    all_to_all x2, blocking collectives, project(): lax.all_to_all(row_major, 'sample', split_axis=1, concat_axis=0, tiled=True)  26.7 us
    dot_general x2, matrix products, expert_apply(): jnp.einsum('scd,df->scf', arrived, gate_up, preferred_element_type=jnp.fl...  21.3 us
    all_to_all x2, starting transfers between devices, run_experts(): lax.all_to_all(outgoing, ('prompt', 'sample'), split_axis=0, concat_axis=...  15.1 us
    reshape x1, local copies, waits for them, and re-layouts, attend(): blocks = piece.reshape(length // block_len, block_len, 2, KVH, HD)  14.3 us
  transfers between devices with their start and end apart: 7, of which 7 were waited for; matrix products, arithmetic and copies ran while one was open for 13% of the time, Pallas kernels for 0%

commit v1 on v0

v1 whole, which is shorter than its diff:
```python
import functools
import math

import jax
import jax.numpy as jnp
from jax import lax
from jax.experimental import pallas as pl
from jax.experimental.pallas import tpu as pltpu
from jax.sharding import PartitionSpec as P

QH = 64
KVH = 4
HD = 128
EPSILON = 1e-06
NEG_LARGE = -1e30
RING = 4
EXP2_SCALE = HD ** (-0.5) * math.log2(math.e)
BF = jnp.bfloat16
F32 = jnp.float32
CUT = 1024


def place():
    index = lax.axis_index("sample")
    return index // 8, (index // 2) % RING, index % 2


def along(axis, shift):
    pairs = []
    for index in range(2 * RING * RING):
        z, y, core = index // 8, (index // 2) % RING, index % 2
        if axis == "z":
            z = (z + shift) % RING
        elif axis == "y":
            y = (y + shift) % RING
        else:
            core = 1 - core
        pairs.append((index, (z * RING + y) * 2 + core))
    return pairs


def shift_to(values, axis, shift=1):
    return lax.ppermute(values, "sample", along(axis, shift))


def ring_sum(chunk, axis):
    ahead2 = chunk(2)
    half = ahead2.shape[0] // 2
    first2, second2 = ahead2[:half].astype(BF), ahead2[half:].astype(BF)
    from_behind = shift_to(first2, axis, 1)
    from_ahead = shift_to(second2, axis, -1)
    ahead1 = chunk(1)
    behind1 = chunk(3)
    got_b = shift_to(ahead1[half:].astype(BF), axis, 1)
    got_c = shift_to(behind1[:half].astype(BF), axis, -1)
    got_a = shift_to((ahead1[:half].astype(F32) + from_behind.astype(F32)).astype(BF), axis, 1)
    got_d = shift_to((behind1[half:].astype(F32) + from_ahead.astype(F32)).astype(BF), axis, -1)
    own = chunk(0).astype(F32)
    return jnp.concatenate(
        [
            own[:half] + got_a.astype(F32) + got_c.astype(F32),
            own[half:] + got_b.astype(F32) + got_d.astype(F32),
        ],
        axis=0,
    )


def attend_kernel(core_ref, own_ref, other_ref, out_ref, score_ref, *, sources, block):
    tile = pl.program_id(0)
    core = core_ref[0]
    rows = sources * 32
    here = pl.ds(tile * sources, sources)
    query = own_ref[here, 0:32, :].reshape(rows, 2 * HD)
    query = jnp.concatenate([query[:, :HD], query[:, HD:]], axis=0)
    wide = query.reshape(2, sources, 2, 16, HD).astype(F32)
    fresh_a = own_ref[here, 32:48, :].astype(F32)
    fresh_b = other_ref[here, 0:16, :].astype(F32)
    step = lax.broadcasted_iota(jnp.int32, (2, sources, 2, 16, 1), 2)
    seen_a, seen_b = core <= step, (1 - core) <= step
    score_a = jnp.sum(wide * fresh_a[None, :, None, :, :HD], axis=-1, keepdims=True)
    score_b = jnp.sum(wide * fresh_b[None, :, None, :, :HD], axis=-1, keepdims=True)
    score_a = jnp.where(seen_a, score_a, NEG_LARGE)
    score_b = jnp.where(seen_b, score_b, NEG_LARGE)
    per = block // 64
    blocks = []
    for ref, offset in ((own_ref, 48), (other_ref, 16)):
        for first in range(0, 32, per):
            blocks.append((ref, offset, first))
    largest = jnp.full((2 * rows, HD), NEG_LARGE, F32)
    for number, (ref, offset, first) in enumerate(blocks):
        keys = ref[first : first + per, offset : offset + 64, 0:HD].reshape(block, HD)
        scores = lax.dot_general(
            query, keys, (((1,), (1,)), ((), ())), preferred_element_type=F32
        )
        score_ref[:, number * block : (number + 1) * block] = scores
        for lane in range(0, block, HD):
            largest = jnp.maximum(largest, scores[:, lane : lane + HD])
    largest = jnp.maximum(
        jnp.max(largest, axis=-1, keepdims=True),
        jnp.maximum(score_a, score_b).reshape(2 * rows, 1),
    )
    summed = jnp.zeros((2 * rows, HD), F32)
    total = jnp.zeros((2 * rows, HD), F32)
    for number, (ref, offset, first) in enumerate(blocks):
        values = ref[first : first + per, offset : offset + 64, HD : 2 * HD].reshape(block, HD)
        weights = jnp.exp2(
            (score_ref[:, number * block : (number + 1) * block] - largest) * EXP2_SCALE
        )
        for lane in range(0, block, HD):
            total = total + weights[:, lane : lane + HD]
        summed = summed + jnp.dot(weights.astype(BF), values, preferred_element_type=F32)
    top = largest.reshape(2, sources, 2, 16, 1)
    weight_a = jnp.where(seen_a, jnp.exp2((score_a - top) * EXP2_SCALE), 0.0)
    weight_b = jnp.where(seen_b, jnp.exp2((score_b - top) * EXP2_SCALE), 0.0)
    row_total = jnp.sum(total, axis=-1, keepdims=True) + (weight_a + weight_b).reshape(2 * rows, 1)
    fresh = (
        weight_a.astype(BF).astype(F32) * fresh_a[None, :, None, :, HD:]
        + weight_b.astype(BF).astype(F32) * fresh_b[None, :, None, :, HD:]
    )
    attended = ((summed + fresh.reshape(2 * rows, HD)) / row_total).astype(BF)
    out_ref[:, 0:HD] = attended[:rows]
    out_ref[:, HD : 2 * HD] = attended[rows:]


def attend(core, own, other):
    sources, block = 8, 512
    return pl.pallas_call(
        functools.partial(attend_kernel, sources=sources, block=block),
        out_shape=jax.ShapeDtypeStruct((1024, 2 * HD), BF),
        grid=(32 // sources,),
        in_specs=[
            pl.BlockSpec(memory_space=pltpu.SMEM),
            pl.BlockSpec((32, 112, 256), lambda i: (0, 0, 0)),
            pl.BlockSpec((32, 80, 256), lambda i: (0, 0, 0)),
        ],
        out_specs=pl.BlockSpec((sources * 32, 2 * HD), lambda i: (i, 0)),
        scratch_shapes=[pltpu.VMEM((sources * 64, 4096), F32)],
        compiler_params=pltpu.CompilerParams(vmem_limit_bytes=40 * 2**20),
        cost_estimate=pl.CostEstimate(
            flops=4 * 2048 * 4096 * HD, bytes_accessed=4 * 2**20, transcendentals=2048 * 4096
        ),
        name="attend",
    )(core, own, other)


def expert_kernel(in_ref, gate_ref, up_ref, down_ref, out_ref, x_ref, act_ref, y_ref, *, parts):
    number = pl.program_id(0)
    near = lax.broadcasted_iota(jnp.int32, (128, 128), 0)
    far = lax.broadcasted_iota(jnp.int32, (128, 128), 1)

    @pl.when(number == 0)
    def _():
        wanted = (near % 32) // 4 * 16 + near // 32 * 4 + near % 4
        order = (wanted == far).astype(BF)
        for group in range(16):
            mixed = jnp.dot(
                order, in_ref[group * 128 : (group + 1) * 128, :], preferred_element_type=F32
            ).astype(BF)
            for cut in range(4):
                x_ref[group * 32 : (group + 1) * 32, cut * CUT : (cut + 1) * CUT] = mixed[
                    cut * 32 : (cut + 1) * 32
                ]

    width = gate_ref.shape[1]
    for part in range(parts):

        @pl.when(number == part)
        def _(part=part):
            gate = jnp.dot(x_ref[...], gate_ref[...], preferred_element_type=F32)
            up = jnp.dot(x_ref[...], up_ref[...], preferred_element_type=F32)
            act_ref[:, part * width : (part + 1) * width] = (
                gate / (1.0 + jnp.exp(-gate)) * up
            ).astype(BF)

    for cut in range(4):

        @pl.when(number == parts + cut)
        def _(cut=cut):
            y = jnp.dot(act_ref[...], down_ref[...], preferred_element_type=F32).astype(BF)
            y_ref[cut] = y

    @pl.when(number == parts + 3)
    def _():
        wanted = (near % 16) // 4 * 32 + near // 16 * 4 + near % 4
        order = (wanted == far).astype(BF)
        for group in range(16):
            together = y_ref[:, group * 32 : (group + 1) * 32, :].reshape(128, CUT)
            out_ref[group * 128 : (group + 1) * 128, :] = jnp.dot(
                order, together, preferred_element_type=F32
            ).astype(BF)


def run_expert(arrived, gate_up, down_weight):
    parts = 3
    width = gate_up.shape[1] // 2 // parts
    clamp = parts - 1
    return pl.pallas_call(
        functools.partial(expert_kernel, parts=parts),
        out_shape=jax.ShapeDtypeStruct(arrived.shape, BF),
        grid=(parts + 4,),
        in_specs=[
            pl.BlockSpec((2048, CUT), lambda i: (0, 0)),
            pl.BlockSpec((4096, width), lambda i: (0, jnp.minimum(i, clamp))),
            pl.BlockSpec((4096, width), lambda i: (0, parts + jnp.minimum(i, clamp))),
            pl.BlockSpec((768, CUT), lambda i: (0, jnp.maximum(i - parts, 0))),
        ],
        out_specs=pl.BlockSpec((2048, CUT), lambda i: (0, 0)),
        scratch_shapes=[
            pltpu.VMEM((512, 4096), BF),
            pltpu.VMEM((512, 768), BF),
            pltpu.VMEM((4, 512, CUT), BF),
        ],
        compiler_params=pltpu.CompilerParams(vmem_limit_bytes=52 * 2**20),
        cost_estimate=pl.CostEstimate(
            flops=2 * 512 * 4096 * 768 * 3, bytes_accessed=27 * 2**20, transcendentals=512 * 768
        ),
        name="expert",
    )(arrived, gate_up, gate_up, down_weight)


def on_device(
    prompt_cache,
    queries,
    new_kv,
    residual,
    out_weight,
    norm_gain,
    gate_up,
    down_weight,
    expert_ids,
    route_weights,
):
    z, y, core = place()
    rows = 32
    to_heads = queries.reshape(rows, 32, 2 * HD).transpose(1, 0, 2)
    fresh = new_kv.reshape(2, 16, 2, KVH, HD).transpose(3, 0, 1, 2, 4).reshape(KVH, 2, 16, 2 * HD)
    cached = prompt_cache.reshape(2, 64, 2, KVH, HD).transpose(3, 0, 1, 2, 4)
    cached = cached.reshape(KVH, 2, 64, 2 * HD)
    both = jnp.concatenate([fresh, cached], axis=2)
    both = jnp.broadcast_to(both[:, None], (KVH, RING, 2, 80, 2 * HD)).reshape(32, 80, 2 * HD)
    sent = jnp.concatenate([to_heads, both], axis=1)
    own = lax.all_to_all(sent, "sample", split_axis=0, concat_axis=0, tiled=True)
    other = shift_to(own[:, 32:, :], "core")
    attended = attend(core.reshape(1).astype(jnp.int32), own, other)

    halves = out_weight.reshape(2 * HD, 2, 2 * CUT)
    mine = lax.dynamic_index_in_dim(halves, core, 1, keepdims=False)
    theirs = lax.dynamic_index_in_dim(halves, 1 - core, 1, keepdims=False)
    weight = jnp.concatenate([mine, shift_to(theirs, "core")], axis=0)
    features = jnp.concatenate([attended, shift_to(attended, "core")], axis=1)
    features = features.reshape(RING, RING, 64, 4 * HD)

    def part_for(column, axis, position):
        def chunk(k):
            picked = lax.dynamic_index_in_dim(
                features, (position + k) % RING, axis, keepdims=False
            ).reshape(256, 4 * HD)
            return jnp.dot(
                picked,
                weight[:, column * CUT : (column + 1) * CUT],
                preferred_element_type=F32,
            ).astype(BF)

        return chunk

    def piece_of(values, position):
        values = values.astype(BF).reshape(RING, 64, CUT)

        def chunk(k):
            return lax.dynamic_index_in_dim(values, (position + k) % RING, 0, keepdims=False)

        return chunk

    first = ring_sum(part_for(0, 1, y), "y")
    second = ring_sum(part_for(1, 0, z), "z")
    first = ring_sum(piece_of(first, z), "z")
    second = ring_sum(piece_of(second, y), "y")
    summed = jnp.stack([first, second]).reshape(2, 2, rows, CUT)
    kept = lax.dynamic_index_in_dim(summed, core, 1, keepdims=False)
    given = lax.dynamic_index_in_dim(summed, 1 - core, 1, keepdims=False)
    got = shift_to(given.astype(BF), "core").astype(F32)
    low = jnp.where(core == 0, kept, got)
    high = jnp.where(core == 0, got, kept)
    quarters = residual.reshape(rows, 4, CUT).transpose(1, 0, 2).astype(F32)
    hidden = quarters + jnp.concatenate([low, high], axis=0)

    moment = jnp.sum(hidden * hidden, axis=(0, 2), keepdims=True) / (4 * CUT)
    normed = (hidden * lax.rsqrt(moment + EPSILON) * norm_gain.reshape(4, 1, CUT)).astype(BF)

    ids = expert_ids.reshape(2, 128)
    row_of = jnp.arange(128, dtype=jnp.int32) // 8
    same = (ids[:, :, None] == ids[:, None, :]) & (row_of[None, :] < row_of[:, None])[None]
    rank = jnp.sum(same.astype(jnp.int32), axis=-1)
    slots = (ids * 4 + jnp.arange(2, dtype=jnp.int32)[:, None] * 2 + rank).reshape(rows, 8)
    hit = slots[:, :, None] == jnp.arange(512, dtype=jnp.int32)
    route = jnp.sum(
        jnp.where(hit, route_weights.reshape(rows, 8, 1), 0.0), axis=1
    )
    chosen = jnp.any(hit, axis=1)
    eye = jnp.eye(4, dtype=bool)
    spread = chosen.T.reshape(128, 1, 4, 1, rows) & eye[None, :, None, :, None]
    spread = spread.astype(BF).reshape(2048, 4 * rows)
    outgoing = jnp.dot(spread, normed.reshape(4 * rows, CUT), preferred_element_type=F32).astype(BF)
    arrived = lax.all_to_all(
        outgoing.reshape(128, 16, CUT), ("prompt", "sample"), split_axis=0, concat_axis=0, tiled=True
    )
    produced = run_expert(arrived.reshape(2048, CUT), gate_up[0], down_weight[0])
    returned = lax.all_to_all(
        produced.reshape(128, 16, CUT), ("prompt", "sample"), split_axis=0, concat_axis=0, tiled=True
    )
    gather = jnp.where(
        eye[:, None, None, :, None], route.reshape(1, rows, 128, 1, 4), 0.0
    ).reshape(4 * rows, 2048)
    coarse = gather.astype(BF)
    fine = (gather - coarse.astype(F32)).astype(BF)
    mixture = jnp.dot(
        jnp.concatenate([coarse, fine], axis=0),
        returned.reshape(2048, CUT),
        preferred_element_type=F32,
    ).reshape(2, 4, rows, CUT)
    total = (hidden + mixture[0] + mixture[1]).astype(BF)
    return total.transpose(1, 0, 2).reshape(2, 16, 4 * CUT)


def solution(mesh):
    in_specs = (
        P("prompt", "sample", None),
        P(None, ("prompt", "sample"), None),
        P(None, ("prompt", "sample"), None),
        P(None, ("prompt", "sample"), None),
        P("sample", None),
        P(),
        P(("prompt", "sample"), None, None),
        P(("prompt", "sample"), None, None),
        P(None, ("prompt", "sample"), None),
        P(None, ("prompt", "sample"), None),
    )
    out_specs = P(None, ("prompt", "sample"), None)
    return jax.shard_map(
        on_device, mesh=mesh, in_specs=in_specs, out_specs=out_specs, check_vma=False
    )
```

time: 481 us -> 287 us (0.60)
  waiting for transfers between devices: 267 us -> 65.1 us
  blocking collectives: 26.7 us -> 93.9 us
  matrix products: 66.3 us -> 8.25 us
  local copies, waits for them, and re-layouts: 68.2 us -> 24.7 us
  Pallas kernels: 0 us -> 35.4 us
  starting transfers between devices: 26.5 us -> 45.6 us
  between operations: 13.5 us -> 0.96 us
    reduce_scatter x2 -> x0, waiting for transfers between devices: 145 us -> none  [project(): lax.psum_scatter(jnp.dot(spread, out_weight, preferred_element_type=jnp.f...]
    all_to_all x2, blocking collectives: 26.7 us -> 93.9 us  [the longest x1 59 us: on_device(): lax.all_to_all(outgoing.reshape(128, 16, CUT), ('prompt', 'sample'), spli...]
    dot_general x30 -> x10, matrix products: 66.3 us -> 8.25 us  [the longest x8 3.54 us: chunk(): jnp.dot(picked, weight[:, column * CUT:(column + 1) * CUT], preferred_ele...]
    all_gather x1 -> x0, waiting for transfers between devices: 53.1 us -> none  [attend(): piece = lax.all_gather(prompt_cache, 'sample', axis=1, tiled=True)]
    ppermute x0 -> x28, starting transfers between devices: none -> 39.2 us  [shift_to(): return lax.ppermute(values, 'sample', along(axis, shift))]
    pallas_call x0 -> x2, Pallas kernels: none -> 35.4 us  [the longest x1 20.8 us: run_expert(): pl.pallas_call(functools.partial(expert_kernel, parts=parts), out_shape=j...]
    reshape x14 -> x8, local copies, waits for them, and re-layouts: 33.5 us -> 3.7 us  [the longest x2 1.32 us: on_device(): cached = prompt_cache.reshape(2, 64, 2, KVH, HD).transpose(3, 0, 1, 2, 4)]
    all_to_all x4 -> x1, waiting for transfers between devices: 68.7 us -> 44.6 us  [on_device(): lax.all_to_all(produced.reshape(128, 16, CUT), ('prompt', 'sample'), spli...]
  transfers between devices with their start and end apart: 7 -> 29, of which waited for: 7 -> 12; matrix products, arithmetic and copies ran while one was open for 13% -> 9% of each run, Pallas kernels for 0% -> 5%
where the time goes in v1:
time: 287 us; the launch traced here: 283 us
  blocking collectives  93.9 us (33%)
  waiting for transfers between devices  65.1 us (23%)
  starting transfers between devices  45.6 us (16%)
  Pallas kernels  35.4 us (12%)
  local copies, waits for them, and re-layouts  24.7 us (9%)
  other arithmetic  9.3 us (3%)
  matrix products  8.25 us (3%)
    all_to_all x1, blocking collectives, on_device(): lax.all_to_all(outgoing.reshape(128, 16, CUT), ('prompt', 'sample'), spli...  59 us
    all_to_all x1, waiting for transfers between devices, on_device(): lax.all_to_all(produced.reshape(128, 16, CUT), ('prompt', 'sample'), spli...  44.6 us
    ppermute x28, starting transfers between devices, shift_to(): return lax.ppermute(values, 'sample', along(axis, shift))  39.2 us
    all_to_all x1, blocking collectives, on_device(): lax.all_to_all(sent, 'sample', split_axis=0, concat_axis=0, tiled=True)  34.9 us
    pallas_call x1, Pallas kernels, run_expert(): pl.pallas_call(functools.partial(expert_kernel, parts=parts), out_shape=j...  20.8 us
    ppermute x28, waiting for transfers between devices, shift_to(): return lax.ppermute(values, 'sample', along(axis, shift))  20.5 us
    pallas_call x1, Pallas kernels, attend(): pl.pallas_call(functools.partial(attend_kernel, sources=sources, block=bl...  14.6 us
    unnamed x19, local copies, waits for them, and re-layouts  6.71 us
  transfers between devices with their start and end apart: 29, of which 12 were waited for; matrix products, arithmetic and copies ran while one was open for 9% of the time, Pallas kernels for 5%

profile of v1, /device:TPU:1, one launch (start us, length us, event | category | flops | bytes accessed | tf_op | source)
XLA Modules:
  0.0 283.2 jit_solution(18340407511871356402)
XLA Ops:
  3.3 34.9 %all_to_all.15.own_ref = bf16[32,112,256]{2,1,0:T(8,128)(2,1)S(1)} all-to-all(bf16[32,112,256]{2,1,0:T(8,128)(2,1)S(1)} %pad_maximum_fusion), channel_id=1, replica_groups=mesh['prompt'=4,'sample'=32] {'sample'}, dimensions={0} | all-to-all | bytes 3670016 | tf_op jit(solution)/shard_map/all_to_all | solution.py:242
  39.9 4.1 %copy.51 = bf16[256,4096]{0,1:T(8,128)(2,1)} copy(bf16[256,4096]{1,0:T(8,128)(2,1)} %param.14) | data formatting | bytes 4194304 | tf_op args[4]
  43.9 3.0 %constant_dynamic-slice_fusion.8 = (bf16[256,1,2048]{0,2,1:T(8,128)(2,1)}, bf16[256,1,2048]{0,2,1:T(8,128)(2,1)}) fusion(bf16[256,2,2048]{0,2,1:T(8,128)(2,1)} %bitcast.155, s32[]{:T(128)S(6)} %select_n.154, s32[]{:T(128)S(6)} %select_n.155), kind=kLoop, calls=%fused_computation.111 | loop fusion | bytes 4194312 | tf_op jit(solution)/shard_map/jit(dynamic_index_in_dim)/dynamic_slice | solution.py:247
  47.0 2.3 copy.53
  52.5 14.6 %attend.1 = bf16[1024,256]{1,0:T(8,128)(2,1)S(1)} custom-call(s32[1]{0:T(128)} %bitcast.1.core_ref, bf16[32,112,256]{2,1,0:T(8,128)(2,1)S(1)} %all_to_all.15.own_ref, bf16[32,80,256]{2,1,0:T(8,128)(2,1)S(1)} %copy-done.1), custom_call_target="tpu_custom_call" | custom-call | flops 4294967296 | bytes 4194304 | tf_op jit(solution)/shard_map/attend/pallas_call | solution.py:127
  74.5 2.8 collective-permute-start.7
  77.5 2.7 collective-permute-start.19
  80.2 2.8 collective-permute-done.3
  83.2 2.8 collective-permute-done.15
  86.5 1.8 collective-permute-done.5
  89.3 2.0 collective-permute-done.6
  91.2 5.6 %collective-permute-done.4 = bf16[128,1024]{1,0:T(8,128)(2,1)S(1)} collective-permute-done((bf16[128,1024]{1,0:T(8,128)(2,1)S(1)}, bf16[128,1024]{1,0:T(8,128)(2,1)S(1)}, u32[]{:S(2)}, u32[]{:S(2)}) %collective-permute-start.4) | collective-permute-done | bytes 262176 | tf_op jit(solution)/shard_map/ppermute | solution.py:43
  98.7 1.8 collective-permute-start.11
  103.4 2.7 collective-permute-start.23
  109.2 1.7 collective-permute-start.14
  112.4 1.5 collective-permute-start.26
  116.2 18.0 %collective-permute-start.27 = (bf16[2,32,1024]{2,1,0:T(8,128)(2,1)S(1)}, bf16[2,32,1024]{2,1,0:T(8,128)(2,1)S(1)}, u32[]{:S(2)}, u32[]{:S(2)}) collective-permute-start(bf16[2,32,1024]{2,1,0:T(8,128)(2,1)S(1)} %fusion.21), channel_id=1, source_target_pairs={{0,1},{1,0},{2,3},{3,2},{4,5},{5,4},{6,7},{7,6},{8,9},{9,8},{10,11... | collective-permute-start | bytes 393224 | tf_op jit(solution)/shard_map/ppermute | solution.py:43
  139.2 59.0 %all_to_all.16 = bf16[128,16,1024]{2,1,0:T(8,128)(2,1)} all-to-all(bf16[128,16,1024]{2,1,0:T(8,128)(2,1)S(1)} %bitcast.150), channel_id=1, replica_groups=mesh['prompt'=4,'sample'=32] {'prompt','sample'}, dimensions={0} | all-to-all | bytes 8388608 | tf_op jit(solution)/shard_map/all_to_all | solution.py:304
  198.3 20.8 %expert.1 = bf16[2048,1024]{1,0:T(8,128)(2,1)} custom-call(bf16[2048,1024]{1,0:T(8,128)(2,1)} %bitcast.152, bf16[4096,1536]{1,0:T(8,128)(2,1)} %bitcast.148, bf16[4096,1536]{1,0:T(8,128)(2,1)} %bitcast.149, bf16[768,4096]{1,0:T(8,128)(2,1)} %bitcast.156), custom_call_target="tpu_custom_call" | custom-call | flops 9663676416 | bytes 28311552 | tf_op jit(solution)/shard_map/expert/pallas_call | solution.py:197
  219.1 6.5 %all-to-all-start.2 = ((bf16[128,16,1024]{2,1,0:T(8,128)(2,1)}), bf16[128,16,1024]{2,1,0:T(8,128)(2,1)}, u32[]{:S(2)}, u32[]{:S(2)}) async-start(bf16[128,16,1024]{2,1,0:T(8,128)(2,1)} %bitcast.151), calls=%async_computation.2 | async-start | bytes 8388608 | tf_op jit(solution)/shard_map/all_to_all | solution.py:308
  226.1 3.4 %broadcast_select_fusion = f32[4,32,128,4,4]{1,0,4,3,2:T(4,128)} fusion(f32[32,128,4]{0,2,1:T(4,128)S(1)} %bitcast.182, pred[4,4]{0,1:T(4,128)(4,1)S(1)} %copy.56), kind=kLoop, calls=%fused_computation.3 | loop fusion | flops 262144 | bytes 1114128 | tf_op jit(solution)/shard_map/jit(_where)/select_n | solution.py:311
  229.5 3.7 %select_n.176 = f32[128,2048]{0,1:T(8,128)S(1)} reshape(f32[4,32,128,4,4]{1,0,4,3,2:T(4,128)} %broadcast_select_fusion) | data formatting | bytes 2097152 | tf_op jit(solution)/shard_map/jit(_where)/select_n | solution.py:311
  233.3 44.6 %all-to-all-done.2 = bf16[128,16,1024]{2,1,0:T(8,128)(2,1)} async-done(((bf16[128,16,1024]{2,1,0:T(8,128)(2,1)}), bf16[128,16,1024]{2,1,0:T(8,128)(2,1)}, u32[]{:S(2)}, u32[]{:S(2)}) %all-to-all-start.2) | async-done | bytes 4194336 | tf_op jit(solution)/shard_map/all_to_all | solution.py:308
  277.9 3.5 %fusion.3 = f32[256,1024]{1,0:T(8,128)S(1)} fusion(bf16[2048,1024]{1,0:T(8,128)(2,1)} %bitcast.52, bf16[128,2048]{0,1:T(8,128)(2,1)S(1)} %get-tuple-element.5, bf16[128,2048]{0,1:T(8,128)(2,1)S(1)} %get-tuple-element.6), kind=kOutput, calls=%fused_computation.19 | convolution fusion | flops 1075838976 | bytes 6291456 | tf_op jit(solution)/shard_map/dot_general | solution.py:316
  (146 shorter events, 36.0 us)
Async XLA Ops:
  39.3 10.8 %collective-permute-start = (bf16[32,80,256]{2,1,0:T(8,128)(2,1)}, bf16[32,80,256]{2,1,0:T(8,128)(2,1)S(1)}, u32[]{:S(2)}, u32[]{:S(2)}) collective-permute-start(bf16[32,80,256]{2,1,0:T(8,128)(2,1)} %slice.208), channel_id=1, source_target_pairs={{0,1},{1,0},{2,3},{3,2},{4,5},{5,4},{6,7},{7,6},{8,9},{9,8},{10,11... | collective-permute-start | bytes 3932168 | tf_op jit(solution)/shard_map/ppermute | solution.py:43
  49.2 19.7 %collective-permute-start.2 = (bf16[256,2048]{1,0:T(8,128)(2,1)}, bf16[256,2048]{1,0:T(8,128)(2,1)}, u32[]{:S(2)}, u32[]{:S(2)}) collective-permute-start(bf16[256,2048]{1,0:T(8,128)(2,1)} %bitcast.183), channel_id=1, source_target_pairs={{0,1},{1,0},{2,3},{3,2},{4,5},{5,4},{6,7},{7,6},{8,9},{9,8},{10,11... | collective-permute-start | bytes 3145736 | tf_op jit(solution)/shard_map/ppermute | solution.py:43
  73.8 9.2 %collective-permute-start.3 = (bf16[128,1024]{1,0:T(8,128)(2,1)S(1)}, bf16[128,1024]{1,0:T(8,128)(2,1)S(1)}, u32[]{:S(2)}, u32[]{:S(2)}) collective-permute-start(bf16[128,1024]{1,0:T(8,128)(2,1)S(1)} %get-tuple-element.33), channel_id=1, source_target_pairs={{0,2},{1,3},{2,4},{3,5},{4,6},{5,7},{6,0},{7,1},{8,10},{9,11},{10,... | collective-permute-start | bytes 786440 | tf_op jit(solution)/shard_map/ppermute | solution.py:43
  74.5 8.5 %collective-permute-start.7 = (bf16[128,1024]{1,0:T(8,128)(2,1)S(1)}, bf16[128,1024]{1,0:T(8,128)(2,1)S(1)}, u32[]{:S(2)}, u32[]{:S(2)}) collective-permute-start(bf16[128,1024]{1,0:T(8,128)(2,1)S(1)} %get-tuple-element.34), channel_id=1, source_target_pairs={{0,6},{1,7},{2,0},{3,1},{4,2},{5,3},{6,4},{7,5},{8,14},{9,15},{10,... | collective-permute-start | bytes 786440 | tf_op jit(solution)/shard_map/ppermute | solution.py:43
  77.5 8.6 %collective-permute-start.15 = (bf16[128,1024]{1,0:T(8,128)(2,1)S(1)}, bf16[128,1024]{1,0:T(8,128)(2,1)S(1)}, u32[]{:S(2)}, u32[]{:S(2)}) collective-permute-start(bf16[128,1024]{1,0:T(8,128)(2,1)S(1)} %get-tuple-element.41), channel_id=1, source_target_pairs={{0,8},{1,9},{2,10},{3,11},{4,12},{5,13},{6,14},{7,15},{8,16},{9,17... | collective-permute-start | bytes 786440 | tf_op jit(solution)/shard_map/ppermute | solution.py:43
  77.5 8.8 %collective-permute-start.19 = (bf16[128,1024]{1,0:T(8,128)(2,1)S(1)}, bf16[128,1024]{1,0:T(8,128)(2,1)S(1)}, u32[]{:S(2)}, u32[]{:S(2)}) collective-permute-start(bf16[128,1024]{1,0:T(8,128)(2,1)S(1)} %get-tuple-element.42), channel_id=1, source_target_pairs={{0,24},{1,25},{2,26},{3,27},{4,28},{5,29},{6,30},{7,31},{8,0},{9,1... | collective-permute-start | bytes 786440 | tf_op jit(solution)/shard_map/ppermute | solution.py:43
  80.2 8.1 %collective-permute-start.5 = (bf16[128,1024]{1,0:T(8,128)(2,1)S(1)}, bf16[128,1024]{1,0:T(8,128)(2,1)S(1)}, u32[]{:S(2)}, u32[]{:S(2)}) collective-permute-start(bf16[128,1024]{1,0:T(8,128)(2,1)S(1)} %slice.214), channel_id=1, source_target_pairs={{0,6},{1,7},{2,0},{3,1},{4,2},{5,3},{6,4},{7,5},{8,14},{9,15},{10,... | collective-permute-start | bytes 786440 | tf_op jit(solution)/shard_map/ppermute | solution.py:43
  83.0 8.2 %collective-permute-start.6 = (bf16[128,1024]{1,0:T(8,128)(2,1)S(1)}, bf16[128,1024]{1,0:T(8,128)(2,1)S(1)}, u32[]{:S(2)}, u32[]{:S(2)}) collective-permute-start(bf16[128,1024]{1,0:T(8,128)(2,1)S(1)} %slice.216), channel_id=1, source_target_pairs={{0,2},{1,3},{2,4},{3,5},{4,6},{5,7},{6,0},{7,1},{8,10},{9,11},{10,... | collective-permute-start | bytes 786440 | tf_op jit(solution)/shard_map/ppermute | solution.py:43
  83.1 13.8 %collective-permute-start.4 = (bf16[128,1024]{1,0:T(8,128)(2,1)S(1)}, bf16[128,1024]{1,0:T(8,128)(2,1)S(1)}, u32[]{:S(2)}, u32[]{:S(2)}) collective-permute-start(bf16[128,1024]{1,0:T(8,128)(2,1)S(1)} %add_convert_fusion.4), channel_id=1, source_target_pairs={{0,2},{1,3},{2,4},{3,5},{4,6},{5,7},{6,0},{7,1},{8,10},{9,11},{10,... | collective-permute-start | bytes 786440 | tf_op jit(solution)/shard_map/ppermute | solution.py:43
  86.0 11.3 %collective-permute-start.8 = (bf16[128,1024]{1,0:T(8,128)(2,1)S(1)}, bf16[128,1024]{1,0:T(8,128)(2,1)S(1)}, u32[]{:S(2)}, u32[]{:S(2)}) collective-permute-start(bf16[128,1024]{1,0:T(8,128)(2,1)S(1)} %add_convert_fusion.3), channel_id=1, source_target_pairs={{0,6},{1,7},{2,0},{3,1},{4,2},{5,3},{6,4},{7,5},{8,14},{9,15},{10,... | collective-permute-start | bytes 786440 | tf_op jit(solution)/shard_map/ppermute | solution.py:43
  86.4 12.4 %collective-permute-start.18 = (bf16[128,1024]{1,0:T(8,128)(2,1)S(1)}, bf16[128,1024]{1,0:T(8,128)(2,1)S(1)}, u32[]{:S(2)}, u32[]{:S(2)}) collective-permute-start(bf16[128,1024]{1,0:T(8,128)(2,1)S(1)} %slice.226), channel_id=1, source_target_pairs={{0,8},{1,9},{2,10},{3,11},{4,12},{5,13},{6,14},{7,15},{8,16},{9,17... | collective-permute-start | bytes 786440 | tf_op jit(solution)/shard_map/ppermute | solution.py:43
  88.3 12.2 %collective-permute-start.17 = (bf16[128,1024]{1,0:T(8,128)(2,1)S(1)}, bf16[128,1024]{1,0:T(8,128)(2,1)S(1)}, u32[]{:S(2)}, u32[]{:S(2)}) collective-permute-start(bf16[128,1024]{1,0:T(8,128)(2,1)S(1)} %slice.224), channel_id=1, source_target_pairs={{0,24},{1,25},{2,26},{3,27},{4,28},{5,29},{6,30},{7,31},{8,0},{9,1... | collective-permute-start | bytes 786440 | tf_op jit(solution)/shard_map/ppermute | solution.py:43
  91.2 9.4 %collective-permute-start.16 = (bf16[128,1024]{1,0:T(8,128)(2,1)S(1)}, bf16[128,1024]{1,0:T(8,128)(2,1)S(1)}, u32[]{:S(2)}, u32[]{:S(2)}) collective-permute-start(bf16[128,1024]{1,0:T(8,128)(2,1)S(1)} %add_convert_fusion.2), channel_id=1, source_target_pairs={{0,8},{1,9},{2,10},{3,11},{4,12},{5,13},{6,14},{7,15},{8,16},{9,17... | collective-permute-start | bytes 786440 | tf_op jit(solution)/shard_map/ppermute | solution.py:43
  96.8 6.1 %collective-permute-start.20 = (bf16[128,1024]{1,0:T(8,128)(2,1)S(1)}, bf16[128,1024]{1,0:T(8,128)(2,1)S(1)}, u32[]{:S(2)}, u32[]{:S(2)}) collective-permute-start(bf16[128,1024]{1,0:T(8,128)(2,1)S(1)} %add_convert_fusion.1), channel_id=1, source_target_pairs={{0,24},{1,25},{2,26},{3,27},{4,28},{5,29},{6,30},{7,31},{8,0},{9,1... | collective-permute-start | bytes 786440 | tf_op jit(solution)/shard_map/ppermute | solution.py:43
  97.7 5.7 %collective-permute-start.9 = (bf16[32,1024]{1,0:T(8,128)(2,1)S(1)}, bf16[32,1024]{1,0:T(8,128)(2,1)S(1)}, u32[]{:S(2)}, u32[]{:S(2)}) collective-permute-start(bf16[32,1024]{1,0:T(8,128)(2,1)S(1)} %get-tuple-element.29), channel_id=1, source_target_pairs={{0,8},{1,9},{2,10},{3,11},{4,12},{5,13},{6,14},{7,15},{8,16},{9,17... | collective-permute-start | bytes 196616 | tf_op jit(solution)/shard_map/ppermute | solution.py:43
  98.7 12.3 %collective-permute-start.11 = (bf16[32,1024]{1,0:T(8,128)(2,1)S(1)}, bf16[32,1024]{1,0:T(8,128)(2,1)S(1)}, u32[]{:S(2)}, u32[]{:S(2)}) collective-permute-start(bf16[32,1024]{1,0:T(8,128)(2,1)S(1)} %get-tuple-element.30), channel_id=1, source_target_pairs={{0,24},{1,25},{2,26},{3,27},{4,28},{5,29},{6,30},{7,31},{8,0},{9,1... | collective-permute-start | bytes 196616 | tf_op jit(solution)/shard_map/ppermute | solution.py:43
  100.5 5.6 %collective-permute-start.13 = (bf16[32,1024]{1,0:T(8,128)(2,1)S(1)}, bf16[32,1024]{1,0:T(8,128)(2,1)S(1)}, u32[]{:S(2)}, u32[]{:S(2)}) collective-permute-start(bf16[32,1024]{1,0:T(8,128)(2,1)S(1)} %get-tuple-element.31), channel_id=1, source_target_pairs={{0,24},{1,25},{2,26},{3,27},{4,28},{5,29},{6,30},{7,31},{8,0},{9,1... | collective-permute-start | bytes 196616 | tf_op jit(solution)/shard_map/ppermute | solution.py:43
  100.6 10.5 %collective-permute-start.12 = (bf16[32,1024]{1,0:T(8,128)(2,1)S(1)}, bf16[32,1024]{1,0:T(8,128)(2,1)S(1)}, u32[]{:S(2)}, u32[]{:S(2)}) collective-permute-start(bf16[32,1024]{1,0:T(8,128)(2,1)S(1)} %get-tuple-element.32), channel_id=1, source_target_pairs={{0,8},{1,9},{2,10},{3,11},{4,12},{5,13},{6,14},{7,15},{8,16},{9,17... | collective-permute-start | bytes 196616 | tf_op jit(solution)/shard_map/ppermute | solution.py:43
  103.3 4.7 %collective-permute-start.21 = (bf16[32,1024]{1,0:T(8,128)(2,1)S(1)}, bf16[32,1024]{1,0:T(8,128)(2,1)S(1)}, u32[]{:S(2)}, u32[]{:S(2)}) collective-permute-start(bf16[32,1024]{1,0:T(8,128)(2,1)S(1)} %get-tuple-element.37), channel_id=1, source_target_pairs={{0,2},{1,3},{2,4},{3,5},{4,6},{5,7},{6,0},{7,1},{8,10},{9,11},{10,... | collective-permute-start | bytes 196616 | tf_op jit(solution)/shard_map/ppermute | solution.py:43
  103.4 10.6 %collective-permute-start.23 = (bf16[32,1024]{1,0:T(8,128)(2,1)S(1)}, bf16[32,1024]{1,0:T(8,128)(2,1)S(1)}, u32[]{:S(2)}, u32[]{:S(2)}) collective-permute-start(bf16[32,1024]{1,0:T(8,128)(2,1)S(1)} %get-tuple-element.38), channel_id=1, source_target_pairs={{0,6},{1,7},{2,0},{3,1},{4,2},{5,3},{6,4},{7,5},{8,14},{9,15},{10,... | collective-permute-start | bytes 196616 | tf_op jit(solution)/shard_map/ppermute | solution.py:43
  109.2 4.7 %collective-permute-start.14 = (bf16[32,1024]{1,0:T(8,128)(2,1)S(1)}, bf16[32,1024]{1,0:T(8,128)(2,1)S(1)}, u32[]{:S(2)}, u32[]{:S(2)}) collective-permute-start(bf16[32,1024]{1,0:T(8,128)(2,1)S(1)} %get-tuple-element.28), channel_id=1, source_target_pairs={{0,24},{1,25},{2,26},{3,27},{4,28},{5,29},{6,30},{7,31},{8,0},{9,1... | collective-permute-start | bytes 196616 | tf_op jit(solution)/shard_map/ppermute | solution.py:43
  111.1 5.0 %collective-permute-start.22 = (bf16[32,1024]{1,0:T(8,128)(2,1)S(1)}, bf16[32,1024]{1,0:T(8,128)(2,1)S(1)}, u32[]{:S(2)}, u32[]{:S(2)}) collective-permute-start(bf16[32,1024]{1,0:T(8,128)(2,1)S(1)} %get-tuple-element.35), channel_id=1, source_target_pairs={{0,2},{1,3},{2,4},{3,5},{4,6},{5,7},{6,0},{7,1},{8,10},{9,11},{10,... | collective-permute-start | bytes 196616 | tf_op jit(solution)/shard_map/ppermute | solution.py:43
  116.2 20.9 %collective-permute-start.27 = (bf16[2,32,1024]{2,1,0:T(8,128)(2,1)S(1)}, bf16[2,32,1024]{2,1,0:T(8,128)(2,1)S(1)}, u32[]{:S(2)}, u32[]{:S(2)}) collective-permute-start(bf16[2,32,1024]{2,1,0:T(8,128)(2,1)S(1)} %fusion.21), channel_id=1, source_target_pairs={{0,1},{1,0},{2,3},{3,2},{4,5},{5,4},{6,7},{7,6},{8,9},{9,8},{10,11... | collective-permute-start | bytes 393224 | tf_op jit(solution)/shard_map/ppermute | solution.py:43
  219.1 58.8 %all-to-all-start.2 = ((bf16[128,16,1024]{2,1,0:T(8,128)(2,1)}), bf16[128,16,1024]{2,1,0:T(8,128)(2,1)}, u32[]{:S(2)}, u32[]{:S(2)}) async-start(bf16[128,16,1024]{2,1,0:T(8,128)(2,1)} %bitcast.151), calls=%async_computation.2 | async-start | bytes 8388608 | tf_op jit(solution)/shard_map/all_to_all | solution.py:308
  (13 other events, 94.3 us)

commit v2 on v1

v2 whole, which is shorter than its diff:
```python
import functools
import math

import jax
import jax.numpy as jnp
from jax import lax
from jax.experimental import pallas as pl
from jax.experimental.pallas import tpu as pltpu
from jax.sharding import PartitionSpec as P

QH = 64
KVH = 4
HD = 128
EPSILON = 1e-06
NEG_LARGE = -1e30
RING = 4
EXP2_SCALE = HD ** (-0.5) * math.log2(math.e)
BF = jnp.bfloat16
F32 = jnp.float32
EXPERT_VMEM = 44
CUT = 1024


def place():
    index = lax.axis_index("sample")
    return index // 8, (index // 2) % RING, index % 2


def move(values, axis, rule):
    pairs = []
    for index in range(2 * RING * RING):
        z, y, core = index // 8, (index // 2) % RING, index % 2
        if axis == "z":
            z = rule(z) % RING
        elif axis == "y":
            y = rule(y) % RING
        else:
            core = rule(core)
        pairs.append((index, (z * RING + y) * 2 + core))
    return lax.ppermute(values, "sample", pairs)


def shift_to(values, axis, shift=1):
    return move(values, axis, lambda at: at + shift)


def to_other_core(values):
    return move(values, "core", lambda at: 1 - at)


def ring_sums(rings):
    halves = []
    for axis, parts in rings:
        half = parts[2].shape[0] // 2
        halves.append(
            (shift_to(parts[2][:half], axis, 1), shift_to(parts[2][half:], axis, -1))
        )
    wholes = []
    for (axis, parts), (behind, ahead) in zip(rings, halves):
        half = behind.shape[0]
        up = jnp.concatenate(
            [(parts[1][:half].astype(F32) + behind.astype(F32)).astype(BF), parts[1][half:]]
        )
        down = jnp.concatenate(
            [parts[3][:half], (parts[3][half:].astype(F32) + ahead.astype(F32)).astype(BF)]
        )
        wholes.append((shift_to(up, axis, 1), shift_to(down, axis, -1)))
    return [
        parts[0].astype(F32) + up.astype(F32) + down.astype(F32)
        for (axis, parts), (up, down) in zip(rings, wholes)
    ]


def halving_sums(rings):
    given = []
    for axis, at, values in rings:
        beside = at ^ 1
        away = jnp.stack([pick(values, beside), pick(values, 3 - beside)]).astype(BF)
        given.append(move(away, axis, lambda index: index ^ 1))
    kept = []
    for (axis, at, values), got in zip(rings, given):
        far = (pick(values, 3 - at) + got[1].astype(F32)).astype(BF)
        kept.append(move(far, axis, lambda index: 3 - index))
    return [
        pick(values, at) + got[0].astype(F32) + last.astype(F32)
        for (axis, at, values), got, last in zip(rings, given, kept)
    ]


def pick(values, index):
    return lax.dynamic_index_in_dim(values, index, 0, keepdims=False)


def pack_kernel(query_ref, fresh_ref, cache_ref, out_ref):
    for z in range(RING):
        for y in range(RING):
            block = y * RING + z
            column = (z * RING + y) * 4 * HD
            out_ref[block, 0:16, :] = query_ref[0, :, column : column + 4 * HD]
            out_ref[block, 16:32, :] = query_ref[1, :, column : column + 4 * HD]
            for side in range(2):
                source = (side * KVH + z) * HD
                for step in range(2):
                    column = (2 * step + side) * HD
                    out_ref[block, 32:48, column : column + HD] = fresh_ref[
                        step, :, source : source + HD
                    ]
                    out_ref[block, 48:112, column : column + HD] = cache_ref[
                        step * 64 : (step + 1) * 64, source : source + HD
                    ]


def pack(queries, new_kv, cache):
    vmem = pl.BlockSpec(memory_space=pltpu.VMEM)
    return pl.pallas_call(
        pack_kernel,
        out_shape=jax.ShapeDtypeStruct((RING * RING, 112, 4 * HD), BF),
        in_specs=[vmem] * 3,
        out_specs=vmem,
        name="pack",
    )(queries, new_kv, cache)


def attend_kernel(
    core_ref, own_ref, other_ref, out_ref, score_ref, value_ref, *, sources, block
):
    tile = pl.program_id(0)
    core = core_ref[0]
    rows = sources * 32
    count = 4 * rows
    here = pl.ds(tile * sources, sources)
    query = own_ref[here, 0:32, :].reshape(rows, 4 * HD)
    query = jnp.concatenate([query[:, head * HD : (head + 1) * HD] for head in range(4)], axis=0)
    per = block // 64
    blocks = []
    for ref, offset in ((own_ref, 48), (other_ref, 0)):
        for column in (0, 2 * HD):
            for first in range(0, 16, per):
                blocks.append((ref, offset, first, column))

    @pl.when(tile == 0)
    def _():
        for number, (ref, offset, first, column) in enumerate(blocks):
            values = ref[first : first + per, offset : offset + 64, column + HD : column + 2 * HD]
            value_ref[:, number * block : (number + 1) * block] = values.reshape(block, HD).T

    fresh = own_ref[here, 32:48, :]
    half = sources * 16
    own_keys, own_values = [
        jnp.concatenate(
            [
                fresh[:, :, step * 2 * HD + begin : step * 2 * HD + begin + HD].reshape(half, HD)
                for step in range(2)
            ],
            axis=0,
        )
        for begin in (0, HD)
    ]
    across = (((1,), (1,)), ((), ()))
    own_scores = lax.dot_general(own_keys, query, across, preferred_element_type=F32)
    key_at = lax.broadcasted_iota(jnp.int32, (2 * half, count), 0)
    row_at = lax.broadcasted_iota(jnp.int32, (2 * half, count), 1) % rows
    same = ((key_at % half) // 16 == row_at // 32) & (key_at % 16 == row_at % 16)
    seen = same & (key_at // half <= (row_at % 32) // 16)
    own_scores = jnp.where(seen, own_scores, NEG_LARGE)

    def fold(values, how):
        return how(values.reshape(values.shape[0] // 8, 8, count), axis=0)

    largest = fold(own_scores, jnp.max)
    for number, (ref, offset, first, column) in enumerate(blocks):
        keys = ref[first : first + per, offset : offset + 64, column : column + HD]
        scores = lax.dot_general(
            keys.reshape(block, HD), query, across, preferred_element_type=F32
        )
        score_ref[number * block : (number + 1) * block, :] = scores
        largest = jnp.maximum(largest, fold(scores, jnp.max))
    largest = jnp.max(largest, axis=0, keepdims=True)
    weights = jnp.exp2((own_scores - largest) * EXP2_SCALE)
    total = fold(weights, jnp.sum)
    summed = jnp.dot(own_values.T, weights.astype(BF), preferred_element_type=F32)
    for number in range(len(blocks)):
        weights = jnp.exp2(
            (score_ref[number * block : (number + 1) * block, :] - largest) * EXP2_SCALE
        )
        total = total + fold(weights, jnp.sum)
        summed = summed + jnp.dot(
            value_ref[:, number * block : (number + 1) * block],
            weights.astype(BF),
            preferred_element_type=F32,
        )
    attended = (summed / jnp.sum(total, axis=0, keepdims=True)).astype(BF).T
    for pair in range(2):
        column = pl.multiple_of(jnp.where(core == pair, 0, 2 * HD), 2 * HD)
        out_ref[:, pl.ds(column, 2 * HD)] = jnp.concatenate(
            [
                attended[2 * pair * rows : (2 * pair + 1) * rows],
                attended[(2 * pair + 1) * rows : (2 * pair + 2) * rows],
            ],
            axis=1,
        )


def attend(core, own, other):
    sources, block = 8, 512
    return pl.pallas_call(
        functools.partial(attend_kernel, sources=sources, block=block),
        out_shape=jax.ShapeDtypeStruct((512, 4 * HD), BF),
        grid=(16 // sources,),
        in_specs=[
            pl.BlockSpec(memory_space=pltpu.SMEM),
            pl.BlockSpec((16, 112, 512), lambda i: (0, 0, 0)),
            pl.BlockSpec((16, 64, 512), lambda i: (0, 0, 0)),
        ],
        out_specs=pl.BlockSpec((sources * 32, 4 * HD), lambda i: (i, 0)),
        scratch_shapes=[pltpu.VMEM((4096, sources * 128), F32), pltpu.VMEM((HD, 4096), BF)],
        compiler_params=pltpu.CompilerParams(vmem_limit_bytes=40 * 2**20),
        cost_estimate=pl.CostEstimate(
            flops=4 * 2048 * 4096 * HD, bytes_accessed=4 * 2**20, transcendentals=2048 * 4096
        ),
        name="attend",
    )(core, own, other)


def project_kernel(place_ref, feature_ref, own_ref, other_ref, *out_refs, order):
    half = 2 * CUT
    for column, outs in ((0, out_refs[: len(order)]), (half, out_refs[len(order) :])):
        columns = slice(column, column + half)
        for k, out_ref in zip(order, outs):
            if column == 0:
                picked = feature_ref[(place_ref[1] + k) % RING]
            else:
                picked = feature_ref[:, (place_ref[0] + k) % RING]
            picked = picked.reshape(128, 4 * HD)
            out_ref[...] = (
                jnp.dot(picked[:, : 2 * HD], own_ref[:, columns], preferred_element_type=F32)
                + jnp.dot(picked[:, 2 * HD :], other_ref[:, columns], preferred_element_type=F32)
            ).astype(BF)


def project(position, features, own, other, order):
    vmem = pl.BlockSpec(memory_space=pltpu.VMEM)
    count = 2 * len(order)
    return pl.pallas_call(
        functools.partial(project_kernel, order=order),
        out_shape=[jax.ShapeDtypeStruct((128, 2 * CUT), BF)] * count,
        in_specs=[pl.BlockSpec(memory_space=pltpu.SMEM), vmem, vmem, vmem],
        out_specs=[vmem] * count,
        compiler_params=pltpu.CompilerParams(vmem_limit_bytes=24 * 2**20),
        cost_estimate=pl.CostEstimate(
            flops=2 * 128 * 512 * 2048 * count, bytes_accessed=5 * 2**20, transcendentals=0
        ),
        name="project",
    )(position, features, own, other)


def dispatch_kernel(
    residual_ref, gain_ref, slot_ref, weight_ref, *refs
):
    sums, (hidden_ref, out_ref, map_ref) = refs[0:2], refs[2:]
    square = jnp.zeros((32, 1), F32)
    for cut in range(4):
        columns = slice(cut * CUT, (cut + 1) * CUT)
        half = slice(cut % 2 * CUT, (cut % 2 + 1) * CUT)
        projected = sums[cut // 2][:, half]
        hidden = projected + residual_ref[:, :, columns].reshape(32, CUT).astype(F32)
        hidden_ref[cut * 32 : (cut + 1) * 32, :] = hidden
        square = square + jnp.sum(hidden * hidden, axis=-1, keepdims=True)
    factor = lax.rsqrt(square / (4 * CUT) + EPSILON)
    normed = jnp.concatenate(
        [
            (
                hidden_ref[cut * 32 : (cut + 1) * 32, :]
                * factor
                * gain_ref[:, cut * CUT : (cut + 1) * CUT]
            ).astype(BF)
            for cut in range(4)
        ],
        axis=0,
    )
    for first in range(0, 2048, 256):
        target = first + lax.broadcasted_iota(jnp.int32, (256, 128), 0)
        hits = jnp.zeros((256, 128), F32)
        value = jnp.zeros((256, 128), F32)
        for choice in range(8):
            hit = target == slot_ref[choice : choice + 1, :]
            hits = jnp.where(hit, 1.0, hits)
            value = jnp.where(hit, weight_ref[choice : choice + 1, :], value)
        out_ref[first : first + 256, :] = jnp.dot(
            hits.astype(BF), normed, preferred_element_type=F32
        ).astype(BF)
        value = value.T
        coarse = value.astype(BF)
        map_ref[0:128, first : first + 256] = coarse
        map_ref[128:256, first : first + 256] = (value - coarse.astype(F32)).astype(BF)


def dispatch(residual, gain, slots, weights, sums):
    vmem = pl.BlockSpec(memory_space=pltpu.VMEM)
    return pl.pallas_call(
        dispatch_kernel,
        out_shape=[
            jax.ShapeDtypeStruct((128, CUT), F32),
            jax.ShapeDtypeStruct((2048, CUT), BF),
            jax.ShapeDtypeStruct((256, 2048), BF),
        ],
        in_specs=[vmem] * 6,
        out_specs=[vmem] * 3,
        compiler_params=pltpu.CompilerParams(vmem_limit_bytes=32 * 2**20),
        cost_estimate=pl.CostEstimate(
            flops=2 * 2048 * 128 * 1024, bytes_accessed=6 * 2**20, transcendentals=32
        ),
        name="dispatch",
    )(residual, gain, slots, weights, *sums)


def combine_kernel(map_ref, returned_ref, hidden_ref, out_ref, held_ref, arrived, *, parts):
    block = 2048 // parts
    copies = []
    for part in range(parts):
        rows = pl.ds(part * block, block)
        copy = pltpu.make_async_copy(returned_ref.at[rows], held_ref.at[rows], arrived.at[part])
        copy.start()
        copies.append(copy)
    total = jnp.zeros((256, CUT), F32)
    for part, copy in enumerate(copies):
        copy.wait()
        rows = slice(part * block, (part + 1) * block)
        total = total + jnp.dot(map_ref[:, rows], held_ref[rows, :], preferred_element_type=F32)
    total = hidden_ref[...] + total[0:128] + total[128:256]
    for cut in range(4):
        out_ref[:, :, cut * CUT : (cut + 1) * CUT] = (
            total[cut * 32 : (cut + 1) * 32].astype(BF).reshape(2, 16, CUT)
        )


def combine(gather, returned, hidden):
    parts = 4
    vmem = pl.BlockSpec(memory_space=pltpu.VMEM)
    return pl.pallas_call(
        functools.partial(combine_kernel, parts=parts),
        out_shape=jax.ShapeDtypeStruct((2, 16, 4 * CUT), BF),
        in_specs=[vmem, pl.BlockSpec(memory_space=pltpu.HBM), vmem],
        out_specs=vmem,
        scratch_shapes=[pltpu.VMEM((2048, CUT), BF), pltpu.SemaphoreType.DMA((parts,))],
        compiler_params=pltpu.CompilerParams(vmem_limit_bytes=32 * 2**20),
        cost_estimate=pl.CostEstimate(
            flops=2 * 256 * 2048 * 1024, bytes_accessed=6 * 2**20, transcendentals=0
        ),
        name="combine",
    )(gather, returned, hidden)


def expert_kernel(
    in_ref, gate_up_hbm, down_hbm, out_ref, w_ref, d_ref, x_ref, act_ref, y_ref, arrived
):
    width = w_ref.shape[3]

    def weights(part):
        return [
            pltpu.make_async_copy(
                gate_up_hbm.at[:, pl.ds(side * 3 * width + part * width, width)],
                w_ref.at[part, side],
                arrived.at[part * 2 + side],
            )
            for side in range(2)
        ]

    def down(cut):
        return pltpu.make_async_copy(
            down_hbm.at[:, pl.ds(cut * CUT, CUT)], d_ref.at[cut], arrived.at[6 + cut]
        )

    coming = weights(0)
    for copy in coming:
        copy.start()
    near = lax.broadcasted_iota(jnp.int32, (128, 128), 0)
    far = lax.broadcasted_iota(jnp.int32, (128, 128), 1)
    to_rows = (near % 32 // 4 * 16 + near // 32 * 4 + near % 4 == far).astype(BF)
    to_blocks = (near % 16 // 4 * 32 + near // 16 * 4 + near % 4 == far).astype(BF)
    for group in range(16):
        mixed = jnp.dot(
            to_rows, in_ref[group * 128 : (group + 1) * 128, :], preferred_element_type=F32
        ).astype(BF)
        for cut in range(4):
            x_ref[group * 32 : (group + 1) * 32, cut * CUT : (cut + 1) * CUT] = mixed[
                cut * 32 : (cut + 1) * 32
            ]
    for part in range(3):
        for copy in coming:
            copy.wait()
        coming = weights(part + 1) if part < 2 else [down(cut) for cut in range(4)]
        for copy in coming:
            copy.start()
        for first in range(0, 512, 256):
            rows = slice(first, first + 256)
            gate = jnp.dot(x_ref[rows], w_ref[part, 0], preferred_element_type=F32)
            up = jnp.dot(x_ref[rows], w_ref[part, 1], preferred_element_type=F32)
            act_ref[rows, part * width : (part + 1) * width] = (
                gate / (1.0 + jnp.exp(-gate)) * up
            ).astype(BF)
    for copy in coming:
        copy.wait()
    for half in range(2):
        rows = slice(half * 256, (half + 1) * 256)
        for cut in range(4):
            y_ref[cut] = jnp.dot(act_ref[rows], d_ref[cut], preferred_element_type=F32).astype(BF)
        for group in range(8):
            together = y_ref[:, group * 32 : (group + 1) * 32, :].reshape(128, CUT)
            first = half * 1024 + group * 128
            out_ref[first : first + 128, :] = jnp.dot(
                to_blocks, together, preferred_element_type=F32
            ).astype(BF)


def run_expert(arrived, gate_up, down_weight):
    width = gate_up.shape[1] // 6
    hbm = pl.BlockSpec(memory_space=pltpu.HBM)
    vmem = pl.BlockSpec(memory_space=pltpu.VMEM)
    return pl.pallas_call(
        expert_kernel,
        out_shape=jax.ShapeDtypeStruct(arrived.shape, BF),
        in_specs=[vmem, hbm, hbm],
        out_specs=vmem,
        scratch_shapes=[
            pltpu.VMEM((3, 2, 4 * CUT, width), BF),
            pltpu.VMEM((4, 3 * width, CUT), BF),
            pltpu.VMEM((512, 4 * CUT), BF),
            pltpu.VMEM((512, 3 * width), BF),
            pltpu.VMEM((4, 256, CUT), BF),
            pltpu.SemaphoreType.DMA((10,)),
        ],
        compiler_params=pltpu.CompilerParams(vmem_limit_bytes=EXPERT_VMEM * 2**20),
        cost_estimate=pl.CostEstimate(
            flops=2 * 512 * 4096 * 768 * 3, bytes_accessed=27 * 2**20, transcendentals=512 * 768
        ),
        name="expert",
    )(arrived, gate_up, down_weight)


def on_device(
    prompt_cache,
    queries,
    new_kv,
    residual,
    out_weight,
    norm_gain,
    gate_up,
    down_weight,
    expert_ids,
    route_weights,
):
    z, y, core = place()
    position = jnp.stack([z, y, core]).astype(jnp.int32)
    everyone = ("sample", "prompt")
    other_weight = to_other_core(out_weight)

    ids = expert_ids.reshape(2, 128)
    ids = ids % 32 * 4 + ids // 32
    row_of = jnp.arange(128, dtype=jnp.int32) // 8
    same = (ids[:, :, None] == ids[:, None, :]) & (row_of[None, :] < row_of[:, None])[None]
    rank = jnp.sum(same.astype(jnp.int32), axis=-1)
    slots = ids * 16 + jnp.arange(2, dtype=jnp.int32)[:, None] * 2 + rank
    slots = slots.reshape(1, 32, 8) + 4 * jnp.arange(4, dtype=jnp.int32)[:, None, None]
    slots = slots.reshape(128, 8)
    weights = jnp.broadcast_to(route_weights.reshape(1, 32, 8), (4, 32, 8)).reshape(128, 8)

    sent = pack(queries, new_kv, prompt_cache[0])
    groups = [
        [2 * (z_at * RING + y_at) + which for y_at in range(RING) for z_at in range(RING)]
        for which in range(2)
    ]
    own = lax.all_to_all(
        sent, "sample", split_axis=0, concat_axis=0, tiled=True, axis_index_groups=groups
    )
    other = to_other_core(own[:, 48:, :])
    features = attend(position[2:], own, other).reshape(RING, RING, 32, 4 * HD)

    farthest = project(position, features, out_weight, other_weight, (2,))
    nearer = project(position, features, out_weight, other_weight, (1, 3, 0))
    parts_y = [nearer[2], nearer[0], farthest[0], nearer[1]]
    parts_z = [nearer[5], nearer[3], farthest[1], nearer[4]]
    sum_y, sum_z = ring_sums([("y", parts_y), ("z", parts_z)])
    sums = halving_sums(
        [
            ("z", z, sum_y.reshape(RING, 32, 2 * CUT)),
            ("y", y, sum_z.reshape(RING, 32, 2 * CUT)),
        ]
    )

    hidden, outgoing, gather = dispatch(
        residual, norm_gain.reshape(1, -1), slots.T, weights.T, sums
    )
    arrived = lax.all_to_all(
        outgoing.reshape(128, 16, CUT), everyone, split_axis=0, concat_axis=0, tiled=True
    )
    produced = run_expert(arrived.reshape(2048, CUT), gate_up[0], down_weight[0])
    returned = lax.all_to_all(
        produced.reshape(128, 16, CUT), everyone, split_axis=0, concat_axis=0, tiled=True
    )
    return combine(gather, returned.reshape(2048, CUT), hidden)


def solution(mesh):
    in_specs = (
        P("prompt", "sample", None),
        P(None, ("prompt", "sample"), None),
        P(None, ("prompt", "sample"), None),
        P(None, ("prompt", "sample"), None),
        P("sample", None),
        P(),
        P(("prompt", "sample"), None, None),
        P(("prompt", "sample"), None, None),
        P(None, ("prompt", "sample"), None),
        P(None, ("prompt", "sample"), None),
    )
    out_specs = P(None, ("prompt", "sample"), None)
    return jax.shard_map(
        on_device, mesh=mesh, in_specs=in_specs, out_specs=out_specs, check_vma=False
    )
```

time: 287 us -> 241 us (0.84); the launches traced: 283 us -> 241 us
  blocking collectives: 93.9 us -> 124 us
  local copies, waits for them, and re-layouts: 24.7 us -> 2.3 us
  starting transfers between devices: 45.6 us -> 24.9 us
  waiting for transfers between devices: 65.1 us -> 47 us
  matrix products: 8.25 us -> 0 us
  other arithmetic: 9.3 us -> 1.4 us
  Pallas kernels: 35.4 us -> 40.6 us
    all_to_all x2, blocking collectives: 93.9 us -> 124 us  [the longest x1 67.1 us: on_device(): lax.all_to_all(outgoing.reshape(128, 16, CUT), everyone, split_axis=0, co...]
    ppermute x28 -> x14, starting transfers between devices: 39.2 us -> 16.3 us  [move(): return lax.ppermute(values, 'sample', pairs)]
    all_to_all x1, waiting for transfers between devices: 44.6 us -> 22.6 us  [on_device(): lax.all_to_all(sent, 'sample', split_axis=0, concat_axis=0, tiled=True, a...]
    dot_general x10 -> x0, matrix products: 8.25 us -> none  [the longest x8 3.54 us: chunk(): jnp.dot(picked, weight[:, column * CUT:(column + 1) * CUT], preferred_ele...]
    pallas_call x1 -> x6, Pallas kernels: 20.8 us -> 28.4 us  [the longest x1 15.6 us: run_expert(): pl.pallas_call(expert_kernel, out_shape=jax.ShapeDtypeStruct(arrived.shap...]
    unnamed x19 -> x13, local copies, waits for them, and re-layouts: 6.71 us -> 0.1 us
    dynamic_slice x5 -> x0, local copies, waits for them, and re-layouts: 6.09 us -> none  [the longest x2 3.65 us: on_device(): mine = lax.dynamic_index_in_dim(halves, core, 1, keepdims=False)]
    ppermute x28 -> x14, waiting for transfers between devices: 20.5 us -> 24.4 us  [move(): return lax.ppermute(values, 'sample', pairs)]
  transfers between devices with their start and end apart: 29 -> 15, of which waited for: 12 -> 8; matrix products, arithmetic and copies ran while one was open for 9% -> 1% of each run, Pallas kernels for 5% -> 6%
where the time goes in v2:
time: 241 us
  blocking collectives  124 us (51%)
  waiting for transfers between devices  47 us (20%)
  Pallas kernels  40.6 us (17%)
  starting transfers between devices  24.9 us (10%)
    all_to_all x1, blocking collectives, on_device(): lax.all_to_all(outgoing.reshape(128, 16, CUT), everyone, split_axis=0, co...  67.1 us
    all_to_all x1, blocking collectives, on_device(): lax.all_to_all(produced.reshape(128, 16, CUT), everyone, split_axis=0, co...  57.1 us
    ppermute x14, waiting for transfers between devices, move(): return lax.ppermute(values, 'sample', pairs)  24.4 us
    all_to_all x1, waiting for transfers between devices, on_device(): lax.all_to_all(sent, 'sample', split_axis=0, concat_axis=0, tiled=True, a...  22.6 us
    ppermute x14, starting transfers between devices, move(): return lax.ppermute(values, 'sample', pairs)  16.3 us
    pallas_call x1, Pallas kernels, run_expert(): pl.pallas_call(expert_kernel, out_shape=jax.ShapeDtypeStruct(arrived.shap...  15.6 us
    pallas_call x1, Pallas kernels, attend(): pl.pallas_call(functools.partial(attend_kernel, sources=sources, block=bl...  12.2 us
    all_to_all x1, starting transfers between devices, on_device(): lax.all_to_all(sent, 'sample', split_axis=0, concat_axis=0, tiled=True, a...  8.6 us
  transfers between devices with their start and end apart: 15, of which 8 were waited for; matrix products, arithmetic and copies ran while one was open for 1% of the time, Pallas kernels for 6%

profile of v2, /device:TPU:1, one launch (start us, length us, event | category | flops | bytes accessed | tf_op | source)
XLA Modules:
  0.0 240.9 jit_solution(4622909310327987442)
XLA Ops:
  0.0 2.6 %pack.1 = bf16[16,112,512]{2,1,0:T(8,128)(2,1)} custom-call(bf16[2,16,8192]{2,1,0:T(8,128)(2,1)} %query_ref.1, bf16[2,16,1024]{2,1,0:T(8,128)(2,1)} %fresh_ref.1, bf16[128,1024]{1,0:T(8,128)(2,1)} %bitcast.47), custom_call_target="tpu_custom_call" | custom-call | tf_op jit(solution)/shard_map/pack/pallas_call | solution.py:115
  2.6 8.6 %all-to-all-start = ((bf16[16,112,512]{2,1,0:T(8,128)(2,1)}), bf16[16,112,512]{2,1,0:T(8,128)(2,1)S(1)}, u32[]{:S(2)}, u32[]{:S(2)}) async-start(bf16[16,112,512]{2,1,0:T(8,128)(2,1)} %pack.1), calls=%async_computation | async-start | bytes 3670016 | tf_op jit(solution)/shard_map/all_to_all | solution.py:473
  12.5 22.6 %all-to-all-done.own_ref = bf16[16,112,512]{2,1,0:T(8,128)(2,1)S(1)} async-done(((bf16[16,112,512]{2,1,0:T(8,128)(2,1)}), bf16[16,112,512]{2,1,0:T(8,128)(2,1)S(1)}, u32[]{:S(2)}, u32[]{:S(2)}) %all-to-all-start) | async-done | bytes 1835040 | tf_op jit(solution)/shard_map/all_to_all | solution.py:473
  35.1 1.1 slice.68
  36.2 4.2 %collective-permute-start = (bf16[16,64,512]{2,1,0:T(8,128)(2,1)}, bf16[16,64,512]{2,1,0:T(8,128)(2,1)S(1)}, u32[]{:S(2)}, u32[]{:S(2)}) collective-permute-start(bf16[16,64,512]{2,1,0:T(8,128)(2,1)} %slice.68), channel_id=1, source_target_pairs={{0,1},{1,0},{2,3},{3,2},{4,5},{5,4},{6,7},{7,6},{8,9},{9,8},{10,11... | collective-permute-start | bytes 3145736 | tf_op jit(solution)/shard_map/ppermute | solution.py:40
  41.5 1.3 collective-permute-done.other_ref
  42.8 12.2 %attend.1 = bf16[512,512]{1,0:T(8,128)(2,1)S(1)} custom-call(s32[1]{0:T(128)} %bitcast.5.core_ref, bf16[16,112,512]{2,1,0:T(8,128)(2,1)S(1)} %all-to-all-done.own_ref, bf16[16,64,512]{2,1,0:T(8,128)(2,1)S(1)} %collective-permute-done.other_ref), custom_call_target="tpu_custom_call" | custom-call | flops 4294967296 | bytes 4194304 | tf_op jit(solution)/shard_map/attend/pallas_call | solution.py:206
  55.0 2.3 project.3
  57.6 2.7 %collective-permute-start.4 = (bf16[64,2048]{1,0:T(8,128)(2,1)S(1)}, bf16[64,2048]{1,0:T(8,128)(2,1)S(1)}, u32[]{:S(2)}, u32[]{:S(2)}) collective-permute-start(bf16[64,2048]{1,0:T(8,128)(2,1)S(1)} %get-tuple-element.34), channel_id=1, source_target_pairs={{0,6},{1,7},{2,0},{3,1},{4,2},{5,3},{6,4},{7,5},{8,14},{9,15},{10,... | collective-permute-start | bytes 786440 | tf_op jit(solution)/shard_map/ppermute | solution.py:40
  60.3 3.4 %project.2 = (bf16[128,2048]{1,0:T(8,128)(2,1)S(1)}, bf16[128,2048]{1,0:T(8,128)(2,1)S(1)}, bf16[128,2048]{1,0:T(8,128)(2,1)S(1)}, bf16[128,2048]{1,0:T(8,128)(2...) custom-call(s32[3]{0:T(128)S(1)} %pad_add_fusion.place_ref, bf16[4,4,32,512]{3,2,1,0:T(8,128)(2,1)S(1)} %bitcast.38, ...), custom_call_target="tpu_custom_call" | custom-call | flops 1610612736 | bytes 5242880 | tf_op jit(solution)/shard_map/project/pallas_call | solution.py:244
  63.8 1.5 collective-permute-start.8
  65.4 1.5 collective-permute-start.11
  66.9 5.0 %collective-permute-done.8 = bf16[64,2048]{1,0:T(8,128)(2,1)S(1)} collective-permute-done((bf16[64,2048]{1,0:T(8,128)(2,1)S(1)}, bf16[64,2048]{1,0:T(8,128)(2,1)S(1)}, u32[]{:S(2)}, u32[]{:S(2)}) %collective-permute-start.8) | collective-permute-done | bytes 262176 | tf_op jit(solution)/shard_map/ppermute | solution.py:40
  72.8 1.2 collective-permute-start.3
  74.0 3.6 %collective-permute-done.11 = bf16[128,2048]{1,0:T(8,128)(2,1)S(1)} collective-permute-done((bf16[128,2048]{1,0:T(8,128)(2,1)S(1)}, bf16[128,2048]{1,0:T(8,128)(2,1)S(1)}, u32[]{:S(2)}, u32[]{:S(2)}) %collective-permute-start.11) | collective-permute-done | bytes 524320 | tf_op jit(solution)/shard_map/ppermute | solution.py:40
  77.6 7.3 %collective-permute-done.9 = bf16[128,2048]{1,0:T(8,128)(2,1)S(1)} collective-permute-done((bf16[128,2048]{1,0:T(8,128)(2,1)S(1)}, bf16[128,2048]{1,0:T(8,128)(2,1)S(1)}, u32[]{:S(2)}, u32[]{:S(2)}) %collective-permute-start.9) | collective-permute-done | bytes 524320 | tf_op jit(solution)/shard_map/ppermute | solution.py:40
  85.7 4.8 %collective-permute-done.12 = bf16[2,32,2048]{2,1,0:T(8,128)(2,1)S(1)} collective-permute-done((bf16[2,32,2048]{2,1,0:T(8,128)(2,1)S(1)}, bf16[2,32,2048]{2,1,0:T(8,128)(2,1)S(1)}, u32[]{:S(2)}, u32[]{:S(2)}) %collective-permute-start.12) | collective-permute-done | bytes 262176 | tf_op jit(solution)/shard_map/ppermute | solution.py:40
  91.3 2.7 %collective-permute-start.7 = (bf16[32,2048]{1,0:T(8,128)(2,1)S(1)}, bf16[32,2048]{1,0:T(8,128)(2,1)S(1)}, u32[]{:S(2)}, u32[]{:S(2)}) collective-permute-start(bf16[32,2048]{1,0:T(8,128)(2,1)S(1)} %fusion), channel_id=1, source_target_pairs={{0,24},{1,25},{2,26},{3,27},{4,28},{5,29},{6,30},{7,31},{8,16},{9,... | collective-permute-start | bytes 393224 | tf_op jit(solution)/shard_map/ppermute | solution.py:40
  94.0 1.6 collective-permute-done.13
  96.5 2.0 dispatch.1
  98.5 67.1 %all_to_all.15 = bf16[128,16,1024]{2,1,0:T(8,128)(2,1)S(1)} all-to-all(bf16[128,16,1024]{2,1,0:T(8,128)(2,1)S(1)} %bitcast.34), channel_id=1, replica_groups=mesh['prompt'=4,'sample'=32] {'sample','prompt'}, dimensions={0} | all-to-all | bytes 8388608 | tf_op jit(solution)/shard_map/all_to_all | solution.py:494
  165.6 15.6 %expert.1 = bf16[2048,1024]{1,0:T(8,128)(2,1)S(1)} custom-call(bf16[2048,1024]{1,0:T(8,128)(2,1)S(1)} %bitcast.35, bf16[4096,1536]{1,0:T(8,128)(2,1)} %bitcast.48, bf16[768,4096]{1,0:T(8,128)(2,1)} %bitcast.49), custom_call_target="tpu_custom_call" | custom-call | flops 9663676416 | bytes 28311552 | tf_op jit(solution)/shard_map/expert/pallas_call | solution.py:420
  181.2 57.1 %all_to_all.16 = bf16[128,16,1024]{2,1,0:T(8,128)(2,1)S(1)} all-to-all(bf16[128,16,1024]{2,1,0:T(8,128)(2,1)S(1)} %bitcast.36), channel_id=1, replica_groups=mesh['prompt'=4,'sample'=32] {'sample','prompt'}, dimensions={0} | all-to-all | bytes 8388608 | tf_op jit(solution)/shard_map/all_to_all | solution.py:498
  238.3 2.5 %combine.1 = bf16[2,16,4096]{2,1,0:T(8,128)(2,1)} custom-call(bf16[256,2048]{1,0:T(8,128)(2,1)S(1)} %get-tuple-element.24.map_ref, bf16[2048,1024]{1,0:T(8,128)(2,1)S(1)} %bitcast.33, f32[128,1024]{1,0:T(8,128)S(1)} %get-tuple-element.26.hidden_ref), custom_call_target="tpu_custom_call" | custom-call | flops 1073741824 | bytes 6291456 | tf_op jit(solution)/shard_map/combine/pallas_call | solution.py:340
  (75 shorter events, 5.9 us)
Async XLA Ops:
  0.0 12.3 %copy-start.3 = (s32[2,16,8]{1,2,0:T(8,128)S(1)}, s32[2,16,8]{1,2,0:T(8,128)}, u32[]{:S(2)}) copy-start(s32[2,16,8]{1,2,0:T(8,128)} %param.18) | copy-start | bytes 3076
  0.0 40.6 %copy-start.4 = (f32[2,16,8]{1,2,0:T(8,128)S(1)}, f32[2,16,8]{1,2,0:T(8,128)}, u32[]{:S(2)}) copy-start(f32[2,16,8]{1,2,0:T(8,128)} %param.19) | copy-start | bytes 3076
  2.6 32.4 %all-to-all-start = ((bf16[16,112,512]{2,1,0:T(8,128)(2,1)}), bf16[16,112,512]{2,1,0:T(8,128)(2,1)S(1)}, u32[]{:S(2)}, u32[]{:S(2)}) async-start(bf16[16,112,512]{2,1,0:T(8,128)(2,1)} %pack.1), calls=%async_computation | async-start | bytes 3670016 | tf_op jit(solution)/shard_map/all_to_all | solution.py:473
  11.2 43.8 %collective-permute-start.1 = (bf16[256,4096]{1,0:T(8,128)(2,1)}, bf16[256,4096]{1,0:T(8,128)(2,1)}, u32[]{:S(2)}, u32[]{:S(2)}) collective-permute-start(bf16[256,4096]{1,0:T(8,128)(2,1)} %own_ref.3), channel_id=1, source_target_pairs={{0,1},{1,0},{2,3},{3,2},{4,5},{5,4},{6,7},{7,6},{8,9},{9,8},{10,11... | collective-permute-start | bytes 6291464 | tf_op jit(solution)/shard_map/ppermute | solution.py:40
  36.2 6.7 %collective-permute-start = (bf16[16,64,512]{2,1,0:T(8,128)(2,1)}, bf16[16,64,512]{2,1,0:T(8,128)(2,1)S(1)}, u32[]{:S(2)}, u32[]{:S(2)}) collective-permute-start(bf16[16,64,512]{2,1,0:T(8,128)(2,1)} %slice.68), channel_id=1, source_target_pairs={{0,1},{1,0},{2,3},{3,2},{4,5},{5,4},{6,7},{7,6},{8,9},{9,8},{10,11... | collective-permute-start | bytes 3145736 | tf_op jit(solution)/shard_map/ppermute | solution.py:40
  41.5 13.5 %copy-start = (bf16[256,4096]{1,0:T(8,128)(2,1)S(1)}, bf16[256,4096]{1,0:T(8,128)(2,1)}, u32[]{:S(2)}) copy-start(bf16[256,4096]{1,0:T(8,128)(2,1)} %own_ref.3) | copy-start | bytes 6291460
  57.4 7.9 %collective-permute-start.10 = (bf16[64,2048]{1,0:T(8,128)(2,1)S(1)}, bf16[64,2048]{1,0:T(8,128)(2,1)S(1)}, u32[]{:S(2)}, u32[]{:S(2)}) collective-permute-start(bf16[64,2048]{1,0:T(8,128)(2,1)S(1)} %get-tuple-element.32), channel_id=1, source_target_pairs={{0,24},{1,25},{2,26},{3,27},{4,28},{5,29},{6,30},{7,31},{8,0},{9,1... | collective-permute-start | bytes 786440 | tf_op jit(solution)/shard_map/ppermute | solution.py:40
  57.5 15.1 %collective-permute-start.2 = (bf16[64,2048]{1,0:T(8,128)(2,1)S(1)}, bf16[64,2048]{1,0:T(8,128)(2,1)S(1)}, u32[]{:S(2)}, u32[]{:S(2)}) collective-permute-start(bf16[64,2048]{1,0:T(8,128)(2,1)S(1)} %get-tuple-element.33), channel_id=1, source_target_pairs={{0,2},{1,3},{2,4},{3,5},{4,6},{5,7},{6,0},{7,1},{8,10},{9,11},{10,... | collective-permute-start | bytes 786440 | tf_op jit(solution)/shard_map/ppermute | solution.py:40
  57.6 14.5 %collective-permute-start.4 = (bf16[64,2048]{1,0:T(8,128)(2,1)S(1)}, bf16[64,2048]{1,0:T(8,128)(2,1)S(1)}, u32[]{:S(2)}, u32[]{:S(2)}) collective-permute-start(bf16[64,2048]{1,0:T(8,128)(2,1)S(1)} %get-tuple-element.34), channel_id=1, source_target_pairs={{0,6},{1,7},{2,0},{3,1},{4,2},{5,3},{6,4},{7,5},{8,14},{9,15},{10,... | collective-permute-start | bytes 786440 | tf_op jit(solution)/shard_map/ppermute | solution.py:40
  63.8 8.1 %collective-permute-start.8 = (bf16[64,2048]{1,0:T(8,128)(2,1)S(1)}, bf16[64,2048]{1,0:T(8,128)(2,1)S(1)}, u32[]{:S(2)}, u32[]{:S(2)}) collective-permute-start(bf16[64,2048]{1,0:T(8,128)(2,1)S(1)} %get-tuple-element.31), channel_id=1, source_target_pairs={{0,8},{1,9},{2,10},{3,11},{4,12},{5,13},{6,14},{7,15},{8,16},{9,17... | collective-permute-start | bytes 786440 | tf_op jit(solution)/shard_map/ppermute | solution.py:40
  65.4 12.2 %collective-permute-start.11 = (bf16[128,2048]{1,0:T(8,128)(2,1)S(1)}, bf16[128,2048]{1,0:T(8,128)(2,1)S(1)}, u32[]{:S(2)}, u32[]{:S(2)}) collective-permute-start(bf16[128,2048]{1,0:T(8,128)(2,1)S(1)} %pad_maximum_fusion.3), channel_id=1, source_target_pairs={{0,24},{1,25},{2,26},{3,27},{4,28},{5,29},{6,30},{7,31},{8,0},{9,1... | collective-permute-start | bytes 1572872 | tf_op jit(solution)/shard_map/ppermute | solution.py:40
  72.1 12.8 %collective-permute-start.9 = (bf16[128,2048]{1,0:T(8,128)(2,1)S(1)}, bf16[128,2048]{1,0:T(8,128)(2,1)S(1)}, u32[]{:S(2)}, u32[]{:S(2)}) collective-permute-start(bf16[128,2048]{1,0:T(8,128)(2,1)S(1)} %pad_maximum_fusion.2), channel_id=1, source_target_pairs={{0,8},{1,9},{2,10},{3,11},{4,12},{5,13},{6,14},{7,15},{8,16},{9,17... | collective-permute-start | bytes 1572872 | tf_op jit(solution)/shard_map/ppermute | solution.py:40
  72.3 13.0 %collective-permute-start.5 = (bf16[128,2048]{1,0:T(8,128)(2,1)S(1)}, bf16[128,2048]{1,0:T(8,128)(2,1)S(1)}, u32[]{:S(2)}, u32[]{:S(2)}) collective-permute-start(bf16[128,2048]{1,0:T(8,128)(2,1)S(1)} %pad_maximum_fusion.1), channel_id=1, source_target_pairs={{0,6},{1,7},{2,0},{3,1},{4,2},{5,3},{6,4},{7,5},{8,14},{9,15},{10,... | collective-permute-start | bytes 1572872 | tf_op jit(solution)/shard_map/ppermute | solution.py:40
  72.8 12.5 %collective-permute-start.3 = (bf16[128,2048]{1,0:T(8,128)(2,1)S(1)}, bf16[128,2048]{1,0:T(8,128)(2,1)S(1)}, u32[]{:S(2)}, u32[]{:S(2)}) collective-permute-start(bf16[128,2048]{1,0:T(8,128)(2,1)S(1)} %pad_maximum_fusion), channel_id=1, source_target_pairs={{0,2},{1,3},{2,4},{3,5},{4,6},{5,7},{6,0},{7,1},{8,10},{9,11},{10,... | collective-permute-start | bytes 1572872 | tf_op jit(solution)/shard_map/ppermute | solution.py:40
  85.1 11.4 %copy-start.1 = (bf16[2,16,4096]{2,1,0:T(8,128)(2,1)S(1)}, bf16[2,16,4096]{2,1,0:T(8,128)(2,1)}, u32[]{:S(2)}) copy-start(bf16[2,16,4096]{2,1,0:T(8,128)(2,1)} %residual_ref.1) | copy-start | bytes 786436
  85.1 11.4 %copy-start.2 = (f32[4096]{0:T(1024)S(1)}, f32[4096]{0:T(1024)}, u32[]{:S(2)}) copy-start(f32[4096]{0:T(1024)} %param.15) | copy-start | bytes 49156
  85.2 5.3 %collective-permute-start.12 = (bf16[2,32,2048]{2,1,0:T(8,128)(2,1)S(1)}, bf16[2,32,2048]{2,1,0:T(8,128)(2,1)S(1)}, u32[]{:S(2)}, u32[]{:S(2)}) collective-permute-start(bf16[2,32,2048]{2,1,0:T(8,128)(2,1)S(1)} %pad_maximum_fusion.5), channel_id=1, source_target_pairs={{0,2},{1,3},{2,0},{3,1},{4,6},{5,7},{6,4},{7,5},{8,10},{9,11},{10,... | collective-permute-start | bytes 786440 | tf_op jit(solution)/shard_map/ppermute | solution.py:40
  85.6 5.7 %collective-permute-start.6 = (bf16[2,32,2048]{2,1,0:T(8,128)(2,1)S(1)}, bf16[2,32,2048]{2,1,0:T(8,128)(2,1)S(1)}, u32[]{:S(2)}, u32[]{:S(2)}) collective-permute-start(bf16[2,32,2048]{2,1,0:T(8,128)(2,1)S(1)} %pad_maximum_fusion.4), channel_id=1, source_target_pairs={{0,8},{1,9},{2,10},{3,11},{4,12},{5,13},{6,14},{7,15},{8,0},{9,1},... | collective-permute-start | bytes 786440 | tf_op jit(solution)/shard_map/ppermute | solution.py:40
  90.6 5.1 %collective-permute-start.13 = (bf16[32,2048]{1,0:T(8,128)(2,1)S(1)}, bf16[32,2048]{1,0:T(8,128)(2,1)S(1)}, u32[]{:S(2)}, u32[]{:S(2)}) collective-permute-start(bf16[32,2048]{1,0:T(8,128)(2,1)S(1)} %fusion.1), channel_id=1, source_target_pairs={{0,6},{1,7},{2,4},{3,5},{4,2},{5,3},{6,0},{7,1},{8,14},{9,15},{10,... | collective-permute-start | bytes 393224 | tf_op jit(solution)/shard_map/ppermute | solution.py:40
  91.3 5.1 %collective-permute-start.7 = (bf16[32,2048]{1,0:T(8,128)(2,1)S(1)}, bf16[32,2048]{1,0:T(8,128)(2,1)S(1)}, u32[]{:S(2)}, u32[]{:S(2)}) collective-permute-start(bf16[32,2048]{1,0:T(8,128)(2,1)S(1)} %fusion), channel_id=1, source_target_pairs={{0,24},{1,25},{2,26},{3,27},{4,28},{5,29},{6,30},{7,31},{8,16},{9,... | collective-permute-start | bytes 393224 | tf_op jit(solution)/shard_map/ppermute | solution.py:40

commit v3 on v2

--- a/solution.py
+++ b/solution.py
@@ -49,25 +49,19 @@
 
 
 def ring_sums(rings):
-    halves = []
-    for axis, parts in rings:
-        half = parts[2].shape[0] // 2
-        halves.append(
-            (shift_to(parts[2][:half], axis, 1), shift_to(parts[2][half:], axis, -1))
-        )
     wholes = []
-    for (axis, parts), (behind, ahead) in zip(rings, halves):
+    for axis, parts, (behind, ahead) in rings:
         half = behind.shape[0]
         up = jnp.concatenate(
             [(parts[1][:half].astype(F32) + behind.astype(F32)).astype(BF), parts[1][half:]]
         )
         down = jnp.concatenate(
-            [parts[3][:half], (parts[3][half:].astype(F32) + ahead.astype(F32)).astype(BF)]
+            [parts[2][:half], (parts[2][half:].astype(F32) + ahead.astype(F32)).astype(BF)]
         )
         wholes.append((shift_to(up, axis, 1), shift_to(down, axis, -1)))
     return [
         parts[0].astype(F32) + up.astype(F32) + down.astype(F32)
-        for (axis, parts), (up, down) in zip(rings, wholes)
+        for (axis, parts, passed), (up, down) in zip(rings, wholes)
     ]
 
 
@@ -75,14 +69,16 @@
     given = []
     for axis, at, values in rings:
         beside = at ^ 1
-        away = jnp.stack([pick(values, beside), pick(values, 3 - beside)]).astype(BF)
+        away = jnp.stack(
+            [pick(values, (beside - at) % RING), pick(values, (3 - beside - at) % RING)]
+        ).astype(BF)
         given.append(move(away, axis, lambda index: index ^ 1))
     kept = []
     for (axis, at, values), got in zip(rings, given):
-        far = (pick(values, 3 - at) + got[1].astype(F32)).astype(BF)
+        far = (pick(values, (3 - 2 * at) % RING) + got[1].astype(F32)).astype(BF)
         kept.append(move(far, axis, lambda index: 3 - index))
     return [
-        pick(values, at) + got[0].astype(F32) + last.astype(F32)
+        values[0] + got[0].astype(F32) + last.astype(F32)
         for (axis, at, values), got, last in zip(rings, given, kept)
     ]
 
@@ -121,15 +117,16 @@
     )(queries, new_kv, cache)
 
 
-def attend_kernel(
-    core_ref, own_ref, other_ref, out_ref, score_ref, value_ref, *, sources, block
-):
-    tile = pl.program_id(0)
-    core = core_ref[0]
+def attend_kernel(place_ref, own_ref, other_ref, *refs, offsets, block):
+    out_ref, score_ref, value_ref = refs[-3:]
+    core = place_ref[2]
+    sources = len(offsets)
     rows = sources * 32
     count = 4 * rows
-    here = pl.ds(tile * sources, sources)
-    query = own_ref[here, 0:32, :].reshape(rows, 4 * HD)
+    at = [
+        (place_ref[1] + dy) % RING * RING + (place_ref[0] + dz) % RING for dy, dz in offsets
+    ]
+    query = jnp.concatenate([own_ref[index, 0:32, :] for index in at], axis=0)
     query = jnp.concatenate([query[:, head * HD : (head + 1) * HD] for head in range(4)], axis=0)
     per = block // 64
     blocks = []
@@ -137,19 +134,16 @@
         for column in (0, 2 * HD):
             for first in range(0, 16, per):
                 blocks.append((ref, offset, first, column))
-
-    @pl.when(tile == 0)
-    def _():
-        for number, (ref, offset, first, column) in enumerate(blocks):
-            values = ref[first : first + per, offset : offset + 64, column + HD : column + 2 * HD]
-            value_ref[:, number * block : (number + 1) * block] = values.reshape(block, HD).T
-
-    fresh = own_ref[here, 32:48, :]
+    for number, (ref, offset, first, column) in enumerate(blocks):
+        values = ref[first : first + per, offset : offset + 64, column + HD : column + 2 * HD]
+        value_ref[:, number * block : (number + 1) * block] = values.reshape(block, HD).T
+
+    fresh = jnp.concatenate([own_ref[index, 32:48, :] for index in at], axis=0)
     half = sources * 16
     own_keys, own_values = [
         jnp.concatenate(
             [
-                fresh[:, :, step * 2 * HD + begin : step * 2 * HD + begin + HD].reshape(half, HD)
+                fresh[:, step * 2 * HD + begin : step * 2 * HD + begin + HD]
                 for step in range(2)
             ],
             axis=0,
@@ -201,57 +195,93 @@
         )
 
 
-def attend(core, own, other):
-    sources, block = 8, 512
-    return pl.pallas_call(
-        functools.partial(attend_kernel, sources=sources, block=block),
-        out_shape=jax.ShapeDtypeStruct((512, 4 * HD), BF),
-        grid=(16 // sources,),
-        in_specs=[
-            pl.BlockSpec(memory_space=pltpu.SMEM),
-            pl.BlockSpec((16, 112, 512), lambda i: (0, 0, 0)),
-            pl.BlockSpec((16, 64, 512), lambda i: (0, 0, 0)),
-        ],
-        out_specs=pl.BlockSpec((sources * 32, 4 * HD), lambda i: (i, 0)),
-        scratch_shapes=[pltpu.VMEM((4096, sources * 128), F32), pltpu.VMEM((HD, 4096), BF)],
-        compiler_params=pltpu.CompilerParams(vmem_limit_bytes=40 * 2**20),
+FIRST = [(2, 0), (2, 1), (2, 2), (2, 3), (0, 2), (1, 2), (3, 2), (0, 0)]
+SECOND = [(dy, dz) for dy in (0, 1, 3) for dz in (0, 1, 3) if (dy, dz) != (0, 0)]
+
+
+def attend(position, own, other, ready=None):
+    first_call = ready is None
+    offsets = FIRST if first_call else SECOND
+    rows = 32 * len(offsets)
+    vmem = pl.BlockSpec(memory_space=pltpu.VMEM)
+    out = jax.ShapeDtypeStruct((rows, 4 * HD), BF)
+    specs = [pl.BlockSpec(memory_space=pltpu.SMEM), vmem, vmem]
+    return pl.pallas_call(
+        functools.partial(attend_kernel, offsets=offsets, block=512),
+        out_shape=out,
+        in_specs=specs if first_call else specs + [vmem],
+        out_specs=vmem,
+        scratch_shapes=[pltpu.VMEM((4096, 4 * rows), F32), pltpu.VMEM((HD, 4096), BF)],
+        compiler_params=pltpu.CompilerParams(vmem_limit_bytes=26 * 2**20),
         cost_estimate=pl.CostEstimate(
-            flops=4 * 2048 * 4096 * HD, bytes_accessed=4 * 2**20, transcendentals=2048 * 4096
+            flops=2 * 2048 * 4096 * HD, bytes_accessed=4 * 2**20, transcendentals=1024 * 4096
         ),
-        name="attend",
-    )(core, own, other)
-
-
-def project_kernel(place_ref, feature_ref, own_ref, other_ref, *out_refs, order):
-    half = 2 * CUT
-    for column, outs in ((0, out_refs[: len(order)]), (half, out_refs[len(order) :])):
-        columns = slice(column, column + half)
-        for k, out_ref in zip(order, outs):
-            if column == 0:
-                picked = feature_ref[(place_ref[1] + k) % RING]
-            else:
-                picked = feature_ref[:, (place_ref[0] + k) % RING]
-            picked = picked.reshape(128, 4 * HD)
-            out_ref[...] = (
-                jnp.dot(picked[:, : 2 * HD], own_ref[:, columns], preferred_element_type=F32)
-                + jnp.dot(picked[:, 2 * HD :], other_ref[:, columns], preferred_element_type=F32)
-            ).astype(BF)
-
-
-def project(position, features, own, other, order):
-    vmem = pl.BlockSpec(memory_space=pltpu.VMEM)
-    count = 2 * len(order)
-    return pl.pallas_call(
-        functools.partial(project_kernel, order=order),
-        out_shape=[jax.ShapeDtypeStruct((128, 2 * CUT), BF)] * count,
-        in_specs=[pl.BlockSpec(memory_space=pltpu.SMEM), vmem, vmem, vmem],
-        out_specs=[vmem] * count,
-        compiler_params=pltpu.CompilerParams(vmem_limit_bytes=24 * 2**20),
+        name="attend_first" if first_call else "attend_second",
+    )(position, own, other, *(() if first_call else (ready,)))
+
+
+def rows_of(feature_refs, offset):
+    which = 0 if offset in FIRST else 1
+    first = 32 * (FIRST, SECOND)[which].index(offset)
+    return feature_refs[which][first : first + 32, :]
+
+
+def partial_sums(own_ref, other_ref, feature_refs, axis, k):
+    columns = slice(axis * 2 * CUT, (axis + 1) * 2 * CUT)
+    offsets = [(k, along) if axis == 0 else (along, k) for along in range(RING)]
+    picked = jnp.concatenate([rows_of(feature_refs, offset) for offset in offsets], axis=0)
+    return (
+        jnp.dot(picked[:, : 2 * HD], own_ref[:, columns], preferred_element_type=F32)
+        + jnp.dot(picked[:, 2 * HD :], other_ref[:, columns], preferred_element_type=F32)
+    ).astype(BF)
+
+
+def project_far_kernel(own_ref, other_ref, feature_ref, *out_refs):
+    for axis in range(2):
+        partial = partial_sums(own_ref, other_ref, [feature_ref], axis, 2)
+        out_refs[2 * axis][...] = partial[:64]
+        out_refs[2 * axis + 1][...] = partial[64:]
+    out_refs[4][...] = jnp.zeros_like(out_refs[4])
+
+
+def project_far(own, other, features):
+    vmem = pl.BlockSpec(memory_space=pltpu.VMEM)
+    return pl.pallas_call(
+        project_far_kernel,
+        out_shape=[jax.ShapeDtypeStruct((64, 2 * CUT), BF)] * 4
+        + [jax.ShapeDtypeStruct((8, HD), F32)],
+        in_specs=[vmem] * 3,
+        out_specs=[vmem] * 5,
+        compiler_params=pltpu.CompilerParams(vmem_limit_bytes=12 * 2**20),
         cost_estimate=pl.CostEstimate(
-            flops=2 * 128 * 512 * 2048 * count, bytes_accessed=5 * 2**20, transcendentals=0
+            flops=4 * 128 * 512 * 2048, bytes_accessed=5 * 2**20, transcendentals=0
         ),
-        name="project",
-    )(position, features, own, other)
+        name="project_far",
+    )(own, other, features)
+
+
+def project_near_kernel(own_ref, other_ref, *refs):
+    out_refs = refs[-6:]
+    for axis in range(2):
+        for number, k in enumerate((0, 1, 3)):
+            out_refs[3 * axis + number][...] = partial_sums(
+                own_ref, other_ref, refs[:2], axis, k
+            )
+
+
+def project_near(own, other, features, ready):
+    vmem = pl.BlockSpec(memory_space=pltpu.VMEM)
+    return pl.pallas_call(
+        project_near_kernel,
+        out_shape=[jax.ShapeDtypeStruct((128, 2 * CUT), BF)] * 6,
+        in_specs=[vmem] * 4 + [pl.BlockSpec(memory_space=pl.ANY)] * len(ready),
+        out_specs=[vmem] * 6,
+        compiler_params=pltpu.CompilerParams(vmem_limit_bytes=12 * 2**20),
+        cost_estimate=pl.CostEstimate(
+            flops=12 * 128 * 512 * 2048, bytes_accessed=5 * 2**20, transcendentals=0
+        ),
+        name="project_near",
+    )(own, other, *features, *ready)
 
 
 def dispatch_kernel(
@@ -474,13 +504,13 @@
         sent, "sample", split_axis=0, concat_axis=0, tiled=True, axis_index_groups=groups
     )
     other = to_other_core(own[:, 48:, :])
-    features = attend(position[2:], own, other).reshape(RING, RING, 32, 4 * HD)
-
-    farthest = project(position, features, out_weight, other_weight, (2,))
-    nearer = project(position, features, out_weight, other_weight, (1, 3, 0))
-    parts_y = [nearer[2], nearer[0], farthest[0], nearer[1]]
-    parts_z = [nearer[5], nearer[3], farthest[1], nearer[4]]
-    sum_y, sum_z = ring_sums([("y", parts_y), ("z", parts_z)])
+    features = attend(position, own, other)
+    *far, token = project_far(out_weight, other_weight, features)
+    steps = (("y", 1), ("y", -1), ("z", 1), ("z", -1))
+    passed = [shift_to(part, *step) for part, step in zip(far, steps)]
+    rest = attend(position, own, other, token)
+    near = project_near(out_weight, other_weight, [features, rest], passed)
+    sum_y, sum_z = ring_sums([("y", near[:3], passed[:2]), ("z", near[3:], passed[2:])])
     sums = halving_sums(
         [
             ("z", z, sum_y.reshape(RING, 32, 2 * CUT)),

time: 241 us -> 240 us (level)
  waiting for transfers between devices: 47 us -> 43.4 us
    ppermute x14, waiting for transfers between devices: 24.4 us -> 20.6 us  [move(): return lax.ppermute(values, 'sample', pairs)]
    pallas_call x3 -> x4, Pallas kernels: 17.9 us -> 19.6 us  [the longest x2 13.1 us: attend(): pl.pallas_call(functools.partial(attend_kernel, offsets=offsets, block=51...]
  transfers between devices with their start and end apart: 15 -> 15, of which waited for: 8 -> 8; matrix products, arithmetic and copies ran while one was open for 1% -> 1% of each run, Pallas kernels for 6% -> 5%
where the time goes in v3:
time: 240 us
  blocking collectives  123 us (51%)
  waiting for transfers between devices  43.4 us (18%)
  Pallas kernels  42.2 us (18%)
  starting transfers between devices  25.7 us (11%)
  local copies, waits for them, and re-layouts  3.61 us (2%)
    all_to_all x1, blocking collectives, on_device(): lax.all_to_all(outgoing.reshape(128, 16, CUT), everyone, split_axis=0, co...  65.8 us
    all_to_all x1, blocking collectives, on_device(): lax.all_to_all(produced.reshape(128, 16, CUT), everyone, split_axis=0, co...  57.1 us
    all_to_all x1, waiting for transfers between devices, on_device(): lax.all_to_all(sent, 'sample', split_axis=0, concat_axis=0, tiled=True, a...  22.8 us
    ppermute x14, waiting for transfers between devices, move(): return lax.ppermute(values, 'sample', pairs)  20.6 us
    ppermute x14, starting transfers between devices, move(): return lax.ppermute(values, 'sample', pairs)  17.1 us
    pallas_call x1, Pallas kernels, run_expert(): pl.pallas_call(expert_kernel, out_shape=jax.ShapeDtypeStruct(arrived.shap...  15.6 us
    pallas_call x2, Pallas kernels, attend(): pl.pallas_call(functools.partial(attend_kernel, offsets=offsets, block=51...  13.1 us
    all_to_all x1, starting transfers between devices, on_device(): lax.all_to_all(sent, 'sample', split_axis=0, concat_axis=0, tiled=True, a...  8.6 us
  transfers between devices with their start and end apart: 15, of which 8 were waited for; matrix products, arithmetic and copies ran while one was open for 1% of the time, Pallas kernels for 5%

profile of v3, /device:TPU:1, one launch (start us, length us, event | category | flops | bytes accessed | tf_op | source)
XLA Modules:
  0.0 239.9 jit_solution(4889535597961775246)
XLA Ops:
  0.0 2.6 %pack.1 = bf16[16,112,512]{2,1,0:T(8,128)(2,1)} custom-call(bf16[2,16,8192]{2,1,0:T(8,128)(2,1)} %query_ref.1, bf16[2,16,1024]{2,1,0:T(8,128)(2,1)} %fresh_ref.1, bf16[128,1024]{1,0:T(8,128)(2,1)} %bitcast.48), custom_call_target="tpu_custom_call" | custom-call | tf_op jit(solution)/shard_map/pack/pallas_call | solution.py:111
  2.6 8.6 %all-to-all-start = ((bf16[16,112,512]{2,1,0:T(8,128)(2,1)}), bf16[16,112,512]{2,1,0:T(8,128)(2,1)S(1)}, u32[]{:S(2)}, u32[]{:S(2)}) async-start(bf16[16,112,512]{2,1,0:T(8,128)(2,1)} %pack.1), calls=%async_computation | async-start | bytes 3670016 | tf_op jit(solution)/shard_map/all_to_all | solution.py:503
  12.3 22.8 %all-to-all-done.own_ref = bf16[16,112,512]{2,1,0:T(8,128)(2,1)S(1)} async-done(((bf16[16,112,512]{2,1,0:T(8,128)(2,1)}), bf16[16,112,512]{2,1,0:T(8,128)(2,1)S(1)}, u32[]{:S(2)}, u32[]{:S(2)}) %all-to-all-start) | async-done | bytes 1835040 | tf_op jit(solution)/shard_map/all_to_all | solution.py:503
  35.1 1.1 slice.62
  36.2 4.2 %collective-permute-start.1 = (bf16[16,64,512]{2,1,0:T(8,128)(2,1)}, bf16[16,64,512]{2,1,0:T(8,128)(2,1)S(1)}, u32[]{:S(2)}, u32[]{:S(2)}) collective-permute-start(bf16[16,64,512]{2,1,0:T(8,128)(2,1)} %slice.62), channel_id=1, source_target_pairs={{0,1},{1,0},{2,3},{3,2},{4,5},{5,4},{6,7},{7,6},{8,9},{9,8},{10,11... | collective-permute-start | bytes 3145736 | tf_op jit(solution)/shard_map/ppermute | solution.py:40
  41.5 1.3 collective-permute-done.1.other_ref
  42.8 6.5 %attend_first.1.feature_ref.refs_0_ = bf16[256,512]{1,0:T(8,128)(2,1)S(1)} custom-call(s32[3]{0:T(128)S(1)} %pad_add_fusion.place_ref, bf16[16,112,512]{2,1,0:T(8,128)(2,1)S(1)} %all-to-all-done.own_ref, bf16[16,64,512]{2,1,0:T(8,128)(2,1)S(1)} %collective-permute-done.1.other_ref), custom_call_target="tpu_custom_call" | custom-call | flops 2147483648 | bytes 4194304 | tf_op jit(solution)/shard_map/attend_first/pallas_call | solution.py:209
  49.4 3.0 %project_far.1 = (bf16[64,2048]{1,0:T(8,128)(2,1)}, bf16[64,2048]{1,0:T(8,128)(2,1)}, bf16[64,2048]{1,0:T(8,128)(2,1)}, bf16[64,2048]{1,0:T(8,128)(2,1)S(1)}, f32[8,128]{1,0:T(8,128)S(1)}) custom-call(bf16[256,4096]{1,0:T(8,128)(2,1)S(1)} %copy-done, bf16[256,4096]{1,0:T(8,128)(2,1)} %collective-permute-done.other_ref, ...), custom_call_target="tpu_custom_call" | custom-call | flops 536870912 | bytes 5242880 | tf_op jit(solution)/shard_map/project_far/pallas_call | solution.py:249
  52.5 2.7 %collective-permute-start.3 = (bf16[64,2048]{1,0:T(8,128)(2,1)}, bf16[64,2048]{1,0:T(8,128)(2,1)S(1)}, u32[]{:S(2)}, u32[]{:S(2)}) collective-permute-start(bf16[64,2048]{1,0:T(8,128)(2,1)} %get-tuple-element.21), channel_id=1, source_target_pairs={{0,6},{1,7},{2,0},{3,1},{4,2},{5,3},{6,4},{7,5},{8,14},{9,15},{10,... | collective-permute-start | bytes 786440 | tf_op jit(solution)/shard_map/ppermute | solution.py:40
  55.4 2.4 collective-permute-start.5
  58.0 1.4 copy-done.3
  59.4 6.5 %attend_second.1.refs_1_ = bf16[256,512]{1,0:T(8,128)(2,1)S(1)} custom-call(s32[3]{0:T(128)S(1)} %pad_add_fusion.place_ref, bf16[16,112,512]{2,1,0:T(8,128)(2,1)S(1)} %all-to-all-done.own_ref, bf16[16,64,512]{2,1,0:T(8,128)(2,1)S(1)} %copy-done.3, f32[8,128]{1,0:T(8,128)S(1)} %get-tuple-element.19.refs_0_), custom_call_target="tpu_custom_call" | custom-call | flops 2147483648 | bytes 4194304 | tf_op jit(solution)/shard_map/attend_second/pallas_call | solution.py:209
  66.0 3.4 %project_near.1 = (bf16[128,2048]{1,0:T(8,128)(2,1)S(1)}, bf16[128,2048]{1,0:T(8,128)(2,1)S(1)}, bf16[128,2048]{1,0:T(8,128)(2,1)S(1)}, bf16[128,2048]{1,0:T(8,1...) custom-call(bf16[256,4096]{1,0:T(8,128)(2,1)S(1)} %copy-done.1, ...), custom_call_target="tpu_custom_call" | custom-call | flops 1610612736 | bytes 5242880 | tf_op jit(solution)/shard_map/project_near/pallas_call | solution.py:274
  69.8 2.7 %collective-permute-start.11 = (bf16[128,2048]{1,0:T(8,128)(2,1)S(1)}, bf16[128,2048]{1,0:T(8,128)(2,1)S(1)}, u32[]{:S(2)}, u32[]{:S(2)}) collective-permute-start(bf16[128,2048]{1,0:T(8,128)(2,1)S(1)} %pad_maximum_fusion.3), channel_id=1, source_target_pairs={{0,24},{1,25},{2,26},{3,27},{4,28},{5,29},{6,30},{7,31},{8,0},{9,1... | collective-permute-start | bytes 1572872 | tf_op jit(solution)/shard_map/ppermute | solution.py:40
  72.9 2.7 %collective-permute-start.7 = (bf16[128,2048]{1,0:T(8,128)(2,1)S(1)}, bf16[128,2048]{1,0:T(8,128)(2,1)S(1)}, u32[]{:S(2)}, u32[]{:S(2)}) collective-permute-start(bf16[128,2048]{1,0:T(8,128)(2,1)S(1)} %pad_maximum_fusion.1), channel_id=1, source_target_pairs={{0,6},{1,7},{2,0},{3,1},{4,2},{5,3},{6,4},{7,5},{8,14},{9,15},{10,... | collective-permute-start | bytes 1572872 | tf_op jit(solution)/shard_map/ppermute | solution.py:40
  75.6 7.3 %collective-permute-done.10 = bf16[128,2048]{1,0:T(8,128)(2,1)S(1)} collective-permute-done((bf16[128,2048]{1,0:T(8,128)(2,1)S(1)}, bf16[128,2048]{1,0:T(8,128)(2,1)S(1)}, u32[]{:S(2)}, u32[]{:S(2)}) %collective-permute-start.10) | collective-permute-done | bytes 524320 | tf_op jit(solution)/shard_map/ppermute | solution.py:40
  83.3 2.1 collective-permute-done.6
  85.8 4.7 %collective-permute-done.12 = bf16[2,32,2048]{2,1,0:T(8,128)(2,1)S(1)} collective-permute-done((bf16[2,32,2048]{2,1,0:T(8,128)(2,1)S(1)}, bf16[2,32,2048]{2,1,0:T(8,128)(2,1)S(1)}, u32[]{:S(2)}, u32[]{:S(2)}) %collective-permute-start.12) | collective-permute-done | bytes 262176 | tf_op jit(solution)/shard_map/ppermute | solution.py:40
  92.0 3.6 %collective-permute-done.13 = bf16[32,2048]{1,0:T(8,128)(2,1)S(1)} collective-permute-done((bf16[32,2048]{1,0:T(8,128)(2,1)S(1)}, bf16[32,2048]{1,0:T(8,128)(2,1)S(1)}, u32[]{:S(2)}, u32[]{:S(2)}) %collective-permute-start.13) | collective-permute-done | bytes 131104 | tf_op jit(solution)/shard_map/ppermute | solution.py:40
  96.7 2.0 dispatch.1
  98.7 65.8 %all_to_all.15 = bf16[128,16,1024]{2,1,0:T(8,128)(2,1)S(1)} all-to-all(bf16[128,16,1024]{2,1,0:T(8,128)(2,1)S(1)} %bitcast.39), channel_id=1, replica_groups=mesh['prompt'=4,'sample'=32] {'sample','prompt'}, dimensions={0} | all-to-all | bytes 8388608 | tf_op jit(solution)/shard_map/all_to_all | solution.py:524
  164.5 15.6 %expert.1 = bf16[2048,1024]{1,0:T(8,128)(2,1)S(1)} custom-call(bf16[2048,1024]{1,0:T(8,128)(2,1)S(1)} %bitcast.40, bf16[4096,1536]{1,0:T(8,128)(2,1)} %bitcast.49, bf16[768,4096]{1,0:T(8,128)(2,1)} %bitcast.50), custom_call_target="tpu_custom_call" | custom-call | flops 9663676416 | bytes 28311552 | tf_op jit(solution)/shard_map/expert/pallas_call | solution.py:450
  180.1 57.1 %all_to_all.16 = bf16[128,16,1024]{2,1,0:T(8,128)(2,1)S(1)} all-to-all(bf16[128,16,1024]{2,1,0:T(8,128)(2,1)S(1)} %bitcast.41), channel_id=1, replica_groups=mesh['prompt'=4,'sample'=32] {'sample','prompt'}, dimensions={0} | all-to-all | bytes 8388608 | tf_op jit(solution)/shard_map/all_to_all | solution.py:528
  237.2 2.5 %combine.1 = bf16[2,16,4096]{2,1,0:T(8,128)(2,1)} custom-call(bf16[256,2048]{1,0:T(8,128)(2,1)S(1)} %get-tuple-element.30.map_ref, bf16[2048,1024]{1,0:T(8,128)(2,1)S(1)} %bitcast.38, f32[128,1024]{1,0:T(8,128)S(1)} %get-tuple-element.32.hidden_ref), custom_call_target="tpu_custom_call" | custom-call | flops 1073741824 | bytes 6291456 | tf_op jit(solution)/shard_map/combine/pallas_call | solution.py:370
  (78 shorter events, 6.7 us)
Async XLA Ops:
  0.0 40.3 %copy-start.6 = (s32[2,16,8]{1,2,0:T(8,128)S(1)}, s32[2,16,8]{1,2,0:T(8,128)}, u32[]{:S(2)}) copy-start(s32[2,16,8]{1,2,0:T(8,128)} %param.18) | copy-start | bytes 3076
  2.6 32.4 %all-to-all-start = ((bf16[16,112,512]{2,1,0:T(8,128)(2,1)}), bf16[16,112,512]{2,1,0:T(8,128)(2,1)S(1)}, u32[]{:S(2)}, u32[]{:S(2)}) async-start(bf16[16,112,512]{2,1,0:T(8,128)(2,1)} %pack.1), calls=%async_computation | async-start | bytes 3670016 | tf_op jit(solution)/shard_map/all_to_all | solution.py:503
  11.2 38.2 %collective-permute-start = (bf16[256,4096]{1,0:T(8,128)(2,1)}, bf16[256,4096]{1,0:T(8,128)(2,1)}, u32[]{:S(2)}, u32[]{:S(2)}) collective-permute-start(bf16[256,4096]{1,0:T(8,128)(2,1)} %own_ref.3), channel_id=1, source_target_pairs={{0,1},{1,0},{2,3},{3,2},{4,5},{5,4},{6,7},{7,6},{8,9},{9,8},{10,11... | collective-permute-start | bytes 6291464 | tf_op jit(solution)/shard_map/ppermute | solution.py:40
  36.2 6.7 %collective-permute-start.1 = (bf16[16,64,512]{2,1,0:T(8,128)(2,1)}, bf16[16,64,512]{2,1,0:T(8,128)(2,1)S(1)}, u32[]{:S(2)}, u32[]{:S(2)}) collective-permute-start(bf16[16,64,512]{2,1,0:T(8,128)(2,1)} %slice.62), channel_id=1, source_target_pairs={{0,1},{1,0},{2,3},{3,2},{4,5},{5,4},{6,7},{7,6},{8,9},{9,8},{10,11... | collective-permute-start | bytes 3145736 | tf_op jit(solution)/shard_map/ppermute | solution.py:40
  41.5 7.9 %copy-start = (bf16[256,4096]{1,0:T(8,128)(2,1)S(1)}, bf16[256,4096]{1,0:T(8,128)(2,1)}, u32[]{:S(2)}) copy-start(bf16[256,4096]{1,0:T(8,128)(2,1)} %own_ref.3) | copy-start | bytes 6291460
  42.8 9.6 %copy-start.2 = (bf16[16,64,512]{2,1,0:T(8,128)(2,1)}, bf16[16,64,512]{2,1,0:T(8,128)(2,1)S(1)}, u32[]{:S(2)}) copy-start(bf16[16,64,512]{2,1,0:T(8,128)(2,1)S(1)} %collective-permute-done.1.other_ref) | copy-start | bytes 3145732
  49.4 8.4 %copy-start.7 = (f32[2,16,8]{1,2,0:T(8,128)S(1)}, f32[2,16,8]{1,2,0:T(8,128)}, u32[]{:S(2)}) copy-start(f32[2,16,8]{1,2,0:T(8,128)} %param.19) | copy-start | bytes 3076
  52.5 13.5 %collective-permute-start.2 = (bf16[64,2048]{1,0:T(8,128)(2,1)}, bf16[64,2048]{1,0:T(8,128)(2,1)S(1)}, u32[]{:S(2)}, u32[]{:S(2)}) collective-permute-start(bf16[64,2048]{1,0:T(8,128)(2,1)} %get-tuple-element.20), channel_id=1, source_target_pairs={{0,2},{1,3},{2,4},{3,5},{4,6},{5,7},{6,0},{7,1},{8,10},{9,11},{10,... | collective-permute-start | bytes 786440 | tf_op jit(solution)/shard_map/ppermute | solution.py:40
  52.5 13.5 %collective-permute-start.3 = (bf16[64,2048]{1,0:T(8,128)(2,1)}, bf16[64,2048]{1,0:T(8,128)(2,1)S(1)}, u32[]{:S(2)}, u32[]{:S(2)}) collective-permute-start(bf16[64,2048]{1,0:T(8,128)(2,1)} %get-tuple-element.21), channel_id=1, source_target_pairs={{0,6},{1,7},{2,0},{3,1},{4,2},{5,3},{6,4},{7,5},{8,14},{9,15},{10,... | collective-permute-start | bytes 786440 | tf_op jit(solution)/shard_map/ppermute | solution.py:40
  55.1 10.8 %collective-permute-start.4 = (bf16[64,2048]{1,0:T(8,128)(2,1)}, bf16[64,2048]{1,0:T(8,128)(2,1)S(1)}, u32[]{:S(2)}, u32[]{:S(2)}) collective-permute-start(bf16[64,2048]{1,0:T(8,128)(2,1)} %get-tuple-element.22), channel_id=1, source_target_pairs={{0,8},{1,9},{2,10},{3,11},{4,12},{5,13},{6,14},{7,15},{8,16},{9,17... | collective-permute-start | bytes 786440 | tf_op jit(solution)/shard_map/ppermute | solution.py:40
  55.4 10.5 %collective-permute-start.5 = (bf16[64,2048]{1,0:T(8,128)(2,1)S(1)}, bf16[64,2048]{1,0:T(8,128)(2,1)S(1)}, u32[]{:S(2)}, u32[]{:S(2)}) collective-permute-start(bf16[64,2048]{1,0:T(8,128)(2,1)S(1)} %get-tuple-element.23), channel_id=1, source_target_pairs={{0,24},{1,25},{2,26},{3,27},{4,28},{5,29},{6,30},{7,31},{8,0},{9,1... | collective-permute-start | bytes 786440 | tf_op jit(solution)/shard_map/ppermute | solution.py:40
  58.0 8.0 %copy-start.1 = (bf16[256,4096]{1,0:T(8,128)(2,1)S(1)}, bf16[256,4096]{1,0:T(8,128)(2,1)}, u32[]{:S(2)}) copy-start(bf16[256,4096]{1,0:T(8,128)(2,1)} %own_ref.3) | copy-start | bytes 6291460
  58.0 1.4 copy-start.3
  69.6 13.2 %collective-permute-start.10 = (bf16[128,2048]{1,0:T(8,128)(2,1)S(1)}, bf16[128,2048]{1,0:T(8,128)(2,1)S(1)}, u32[]{:S(2)}, u32[]{:S(2)}) collective-permute-start(bf16[128,2048]{1,0:T(8,128)(2,1)S(1)} %pad_maximum_fusion.2), channel_id=1, source_target_pairs={{0,8},{1,9},{2,10},{3,11},{4,12},{5,13},{6,14},{7,15},{8,16},{9,17... | collective-permute-start | bytes 1572872 | tf_op jit(solution)/shard_map/ppermute | solution.py:40
  69.8 13.1 %collective-permute-start.11 = (bf16[128,2048]{1,0:T(8,128)(2,1)S(1)}, bf16[128,2048]{1,0:T(8,128)(2,1)S(1)}, u32[]{:S(2)}, u32[]{:S(2)}) collective-permute-start(bf16[128,2048]{1,0:T(8,128)(2,1)S(1)} %pad_maximum_fusion.3), channel_id=1, source_target_pairs={{0,24},{1,25},{2,26},{3,27},{4,28},{5,29},{6,30},{7,31},{8,0},{9,1... | collective-permute-start | bytes 1572872 | tf_op jit(solution)/shard_map/ppermute | solution.py:40
  72.7 12.6 %collective-permute-start.6 = (bf16[128,2048]{1,0:T(8,128)(2,1)S(1)}, bf16[128,2048]{1,0:T(8,128)(2,1)S(1)}, u32[]{:S(2)}, u32[]{:S(2)}) collective-permute-start(bf16[128,2048]{1,0:T(8,128)(2,1)S(1)} %pad_maximum_fusion), channel_id=1, source_target_pairs={{0,2},{1,3},{2,4},{3,5},{4,6},{5,7},{6,0},{7,1},{8,10},{9,11},{10,... | collective-permute-start | bytes 1572872 | tf_op jit(solution)/shard_map/ppermute | solution.py:40
  72.9 12.5 %collective-permute-start.7 = (bf16[128,2048]{1,0:T(8,128)(2,1)S(1)}, bf16[128,2048]{1,0:T(8,128)(2,1)S(1)}, u32[]{:S(2)}, u32[]{:S(2)}) collective-permute-start(bf16[128,2048]{1,0:T(8,128)(2,1)S(1)} %pad_maximum_fusion.1), channel_id=1, source_target_pairs={{0,6},{1,7},{2,0},{3,1},{4,2},{5,3},{6,4},{7,5},{8,14},{9,15},{10,... | collective-permute-start | bytes 1572872 | tf_op jit(solution)/shard_map/ppermute | solution.py:40
  83.1 13.6 %copy-start.4 = (bf16[2,16,4096]{2,1,0:T(8,128)(2,1)S(1)}, bf16[2,16,4096]{2,1,0:T(8,128)(2,1)}, u32[]{:S(2)}) copy-start(bf16[2,16,4096]{2,1,0:T(8,128)(2,1)} %residual_ref.1) | copy-start | bytes 786436
  83.1 13.6 %copy-start.5 = (f32[4096]{0:T(1024)S(1)}, f32[4096]{0:T(1024)}, u32[]{:S(2)}) copy-start(f32[4096]{0:T(1024)} %param.15) | copy-start | bytes 49156
  83.2 7.3 %collective-permute-start.12 = (bf16[2,32,2048]{2,1,0:T(8,128)(2,1)S(1)}, bf16[2,32,2048]{2,1,0:T(8,128)(2,1)S(1)}, u32[]{:S(2)}, u32[]{:S(2)}) collective-permute-start(bf16[2,32,2048]{2,1,0:T(8,128)(2,1)S(1)} %pad_maximum_fusion.5), channel_id=1, source_target_pairs={{0,2},{1,3},{2,0},{3,1},{4,6},{5,7},{6,4},{7,5},{8,10},{9,11},{10,... | collective-permute-start | bytes 786440 | tf_op jit(solution)/shard_map/ppermute | solution.py:40
  85.7 5.6 %collective-permute-start.8 = (bf16[2,32,2048]{2,1,0:T(8,128)(2,1)S(1)}, bf16[2,32,2048]{2,1,0:T(8,128)(2,1)S(1)}, u32[]{:S(2)}, u32[]{:S(2)}) collective-permute-start(bf16[2,32,2048]{2,1,0:T(8,128)(2,1)S(1)} %pad_maximum_fusion.4), channel_id=1, source_target_pairs={{0,8},{1,9},{2,10},{3,11},{4,12},{5,13},{6,14},{7,15},{8,0},{9,1},... | collective-permute-start | bytes 786440 | tf_op jit(solution)/shard_map/ppermute | solution.py:40
  90.5 5.1 %collective-permute-start.13 = (bf16[32,2048]{1,0:T(8,128)(2,1)S(1)}, bf16[32,2048]{1,0:T(8,128)(2,1)S(1)}, u32[]{:S(2)}, u32[]{:S(2)}) collective-permute-start(bf16[32,2048]{1,0:T(8,128)(2,1)S(1)} %fusion.3), channel_id=1, source_target_pairs={{0,6},{1,7},{2,4},{3,5},{4,2},{5,3},{6,0},{7,1},{8,14},{9,15},{10,... | collective-permute-start | bytes 393224 | tf_op jit(solution)/shard_map/ppermute | solution.py:40
  91.3 5.3 %collective-permute-start.9 = (bf16[32,2048]{1,0:T(8,128)(2,1)S(1)}, bf16[32,2048]{1,0:T(8,128)(2,1)S(1)}, u32[]{:S(2)}, u32[]{:S(2)}) collective-permute-start(bf16[32,2048]{1,0:T(8,128)(2,1)S(1)} %fusion.2), channel_id=1, source_target_pairs={{0,24},{1,25},{2,26},{3,27},{4,28},{5,29},{6,30},{7,31},{8,16},{9,... | collective-permute-start | bytes 393224 | tf_op jit(solution)/shard_map/ppermute | solution.py:40

commit v4 on v3

--- a/solution.py
+++ b/solution.py
@@ -117,8 +117,10 @@
     )(queries, new_kv, cache)
 
 
-def attend_kernel(place_ref, own_ref, other_ref, *refs, offsets, block):
-    out_ref, score_ref, value_ref = refs[-3:]
+def attend_kernel(place_ref, own_ref, other_hbm, *refs, offsets, block):
+    out_ref, score_ref, value_ref, other_ref, arrived = refs[-5:]
+    coming = pltpu.make_async_copy(other_hbm, other_ref, arrived.at[0])
+    coming.start()
     core = place_ref[2]
     sources = len(offsets)
     rows = sources * 32
@@ -134,9 +136,6 @@
         for column in (0, 2 * HD):
             for first in range(0, 16, per):
                 blocks.append((ref, offset, first, column))
-    for number, (ref, offset, first, column) in enumerate(blocks):
-        values = ref[first : first + per, offset : offset + 64, column + HD : column + 2 * HD]
-        value_ref[:, number * block : (number + 1) * block] = values.reshape(block, HD).T
 
     fresh = jnp.concatenate([own_ref[index, 32:48, :] for index in at], axis=0)
     half = sources * 16
@@ -163,12 +162,17 @@
 
     largest = fold(own_scores, jnp.max)
     for number, (ref, offset, first, column) in enumerate(blocks):
+        if number == len(blocks) // 2:
+            coming.wait()
         keys = ref[first : first + per, offset : offset + 64, column : column + HD]
         scores = lax.dot_general(
             keys.reshape(block, HD), query, across, preferred_element_type=F32
         )
         score_ref[number * block : (number + 1) * block, :] = scores
         largest = jnp.maximum(largest, fold(scores, jnp.max))
+    for number, (ref, offset, first, column) in enumerate(blocks):
+        values = ref[first : first + per, offset : offset + 64, column + HD : column + 2 * HD]
+        value_ref[:, number * block : (number + 1) * block] = values.reshape(block, HD).T
     largest = jnp.max(largest, axis=0, keepdims=True)
     weights = jnp.exp2((own_scores - largest) * EXP2_SCALE)
     total = fold(weights, jnp.sum)
@@ -205,13 +209,18 @@
     rows = 32 * len(offsets)
     vmem = pl.BlockSpec(memory_space=pltpu.VMEM)
     out = jax.ShapeDtypeStruct((rows, 4 * HD), BF)
-    specs = [pl.BlockSpec(memory_space=pltpu.SMEM), vmem, vmem]
+    specs = [pl.BlockSpec(memory_space=pltpu.SMEM), vmem, pl.BlockSpec(memory_space=pl.ANY)]
     return pl.pallas_call(
         functools.partial(attend_kernel, offsets=offsets, block=512),
         out_shape=out,
         in_specs=specs if first_call else specs + [vmem],
         out_specs=vmem,
-        scratch_shapes=[pltpu.VMEM((4096, 4 * rows), F32), pltpu.VMEM((HD, 4096), BF)],
+        scratch_shapes=[
+            pltpu.VMEM((4096, 4 * rows), F32),
+            pltpu.VMEM((HD, 4096), BF),
+            pltpu.VMEM((16, 64, 4 * HD), BF),
+            pltpu.SemaphoreType.DMA((1,)),
+        ],
         compiler_params=pltpu.CompilerParams(vmem_limit_bytes=26 * 2**20),
         cost_estimate=pl.CostEstimate(
             flops=2 * 2048 * 4096 * HD, bytes_accessed=4 * 2**20, transcendentals=1024 * 4096

time: 240 us -> 241 us (level)
  transfers between devices with their start and end apart: 15 -> 15, of which waited for: 8 -> 8; matrix products, arithmetic and copies ran while one was open for 1% -> 1% of each run, Pallas kernels for 5% -> 6%
where the time goes in v4:
time: 241 us; the launch traced here: 240 us
  blocking collectives  123 us (51%)
  waiting for transfers between devices  43.4 us (18%)
  Pallas kernels  42.8 us (18%)
  starting transfers between devices  25.7 us (11%)
  local copies, waits for them, and re-layouts  3.61 us (1%)
    all_to_all x1, blocking collectives, on_device(): lax.all_to_all(outgoing.reshape(128, 16, CUT), everyone, split_axis=0, co...  65.8 us
    all_to_all x1, blocking collectives, on_device(): lax.all_to_all(produced.reshape(128, 16, CUT), everyone, split_axis=0, co...  57.1 us
    all_to_all x1, waiting for transfers between devices, on_device(): lax.all_to_all(sent, 'sample', split_axis=0, concat_axis=0, tiled=True, a...  22.8 us
    ppermute x14, waiting for transfers between devices, move(): return lax.ppermute(values, 'sample', pairs)  20.6 us
    ppermute x14, starting transfers between devices, move(): return lax.ppermute(values, 'sample', pairs)  17.1 us
    pallas_call x1, Pallas kernels, run_expert(): pl.pallas_call(expert_kernel, out_shape=jax.ShapeDtypeStruct(arrived.shap...  15.6 us
    pallas_call x2, Pallas kernels, attend(): pl.pallas_call(functools.partial(attend_kernel, offsets=offsets, block=51...  13.6 us
    all_to_all x1, starting transfers between devices, on_device(): lax.all_to_all(sent, 'sample', split_axis=0, concat_axis=0, tiled=True, a...  8.6 us
  transfers between devices with their start and end apart: 15, of which 8 were waited for; matrix products, arithmetic and copies ran while one was open for 1% of the time, Pallas kernels for 6%

profile of v4, /device:TPU:1, one launch (start us, length us, event | category | flops | bytes accessed | tf_op | source)
XLA Modules:
  0.0 240.4 jit_solution(8906560164471636272)
XLA Ops:
  0.0 2.6 %pack.1 = bf16[16,112,512]{2,1,0:T(8,128)(2,1)} custom-call(bf16[2,16,8192]{2,1,0:T(8,128)(2,1)} %query_ref.1, bf16[2,16,1024]{2,1,0:T(8,128)(2,1)} %fresh_ref.1, bf16[128,1024]{1,0:T(8,128)(2,1)} %bitcast.48), custom_call_target="tpu_custom_call" | custom-call | tf_op jit(solution)/shard_map/pack/pallas_call | solution.py:111
  2.6 8.6 %all-to-all-start = ((bf16[16,112,512]{2,1,0:T(8,128)(2,1)}), bf16[16,112,512]{2,1,0:T(8,128)(2,1)S(1)}, u32[]{:S(2)}, u32[]{:S(2)}) async-start(bf16[16,112,512]{2,1,0:T(8,128)(2,1)} %pack.1), calls=%async_computation | async-start | bytes 3670016 | tf_op jit(solution)/shard_map/all_to_all | solution.py:512
  12.3 22.8 %all-to-all-done.own_ref = bf16[16,112,512]{2,1,0:T(8,128)(2,1)S(1)} async-done(((bf16[16,112,512]{2,1,0:T(8,128)(2,1)}), bf16[16,112,512]{2,1,0:T(8,128)(2,1)S(1)}, u32[]{:S(2)}, u32[]{:S(2)}) %all-to-all-start) | async-done | bytes 1835040 | tf_op jit(solution)/shard_map/all_to_all | solution.py:512
  35.1 1.1 slice.62
  36.2 4.2 %collective-permute-start.1 = (bf16[16,64,512]{2,1,0:T(8,128)(2,1)}, bf16[16,64,512]{2,1,0:T(8,128)(2,1)S(1)}, u32[]{:S(2)}, u32[]{:S(2)}) collective-permute-start(bf16[16,64,512]{2,1,0:T(8,128)(2,1)} %slice.62), channel_id=1, source_target_pairs={{0,1},{1,0},{2,3},{3,2},{4,5},{5,4},{6,7},{7,6},{8,9},{9,8},{10,11... | collective-permute-start | bytes 3145736 | tf_op jit(solution)/shard_map/ppermute | solution.py:40
  41.5 1.3 collective-permute-done.1.other_hbm
  42.8 6.8 %attend_first.1.feature_ref.refs_0_ = bf16[256,512]{1,0:T(8,128)(2,1)S(1)} custom-call(s32[3]{0:T(128)S(1)} %pad_add_fusion.place_ref, bf16[16,112,512]{2,1,0:T(8,128)(2,1)S(1)} %all-to-all-done.own_ref, bf16[16,64,512]{2,1,0:T(8,128)(2,1)S(1)} %collective-permute-done.1.other_hbm), custom_call_target="tpu_custom_call" | custom-call | flops 2147483648 | bytes 4194304 | tf_op jit(solution)/shard_map/attend_first/pallas_call | solution.py:213
  49.7 3.0 %project_far.1 = (bf16[64,2048]{1,0:T(8,128)(2,1)}, bf16[64,2048]{1,0:T(8,128)(2,1)}, bf16[64,2048]{1,0:T(8,128)(2,1)}, bf16[64,2048]{1,0:T(8,128)(2,1)S(1)}, f32[8,128]{1,0:T(8,128)S(1)}) custom-call(bf16[256,4096]{1,0:T(8,128)(2,1)S(1)} %copy-done, bf16[256,4096]{1,0:T(8,128)(2,1)} %collective-permute-done.other_ref, ...), custom_call_target="tpu_custom_call" | custom-call | flops 536870912 | bytes 5242880 | tf_op jit(solution)/shard_map/project_far/pallas_call | solution.py:258
  52.7 2.7 %collective-permute-start.3 = (bf16[64,2048]{1,0:T(8,128)(2,1)}, bf16[64,2048]{1,0:T(8,128)(2,1)S(1)}, u32[]{:S(2)}, u32[]{:S(2)}) collective-permute-start(bf16[64,2048]{1,0:T(8,128)(2,1)} %get-tuple-element.21), channel_id=1, source_target_pairs={{0,6},{1,7},{2,0},{3,1},{4,2},{5,3},{6,4},{7,5},{8,14},{9,15},{10,... | collective-permute-start | bytes 786440 | tf_op jit(solution)/shard_map/ppermute | solution.py:40
  55.7 2.4 %collective-permute-start.5 = (bf16[64,2048]{1,0:T(8,128)(2,1)S(1)}, bf16[64,2048]{1,0:T(8,128)(2,1)S(1)}, u32[]{:S(2)}, u32[]{:S(2)}) collective-permute-start(bf16[64,2048]{1,0:T(8,128)(2,1)S(1)} %get-tuple-element.23), channel_id=1, source_target_pairs={{0,24},{1,25},{2,26},{3,27},{4,28},{5,29},{6,30},{7,31},{8,0},{9,1... | collective-permute-start | bytes 786440 | tf_op jit(solution)/shard_map/ppermute | solution.py:40
  58.3 1.4 copy-done.3
  59.6 6.8 %attend_second.1.refs_1_ = bf16[256,512]{1,0:T(8,128)(2,1)S(1)} custom-call(s32[3]{0:T(128)S(1)} %pad_add_fusion.place_ref, bf16[16,112,512]{2,1,0:T(8,128)(2,1)S(1)} %all-to-all-done.own_ref, bf16[16,64,512]{2,1,0:T(8,128)(2,1)S(1)} %copy-done.3, f32[8,128]{1,0:T(8,128)S(1)} %get-tuple-element.19.refs_0_), custom_call_target="tpu_custom_call" | custom-call | flops 2147483648 | bytes 4194304 | tf_op jit(solution)/shard_map/attend_second/pallas_call | solution.py:213
  66.5 3.4 %project_near.1 = (bf16[128,2048]{1,0:T(8,128)(2,1)S(1)}, bf16[128,2048]{1,0:T(8,128)(2,1)S(1)}, bf16[128,2048]{1,0:T(8,128)(2,1)S(1)}, bf16[128,2048]{1,0:T(8,1...) custom-call(bf16[256,4096]{1,0:T(8,128)(2,1)S(1)} %copy-done.1, ...), custom_call_target="tpu_custom_call" | custom-call | flops 1610612736 | bytes 5242880 | tf_op jit(solution)/shard_map/project_near/pallas_call | solution.py:283
  70.3 2.7 %collective-permute-start.11 = (bf16[128,2048]{1,0:T(8,128)(2,1)S(1)}, bf16[128,2048]{1,0:T(8,128)(2,1)S(1)}, u32[]{:S(2)}, u32[]{:S(2)}) collective-permute-start(bf16[128,2048]{1,0:T(8,128)(2,1)S(1)} %pad_maximum_fusion.3), channel_id=1, source_target_pairs={{0,24},{1,25},{2,26},{3,27},{4,28},{5,29},{6,30},{7,31},{8,0},{9,1... | collective-permute-start | bytes 1572872 | tf_op jit(solution)/shard_map/ppermute | solution.py:40
  73.4 2.7 %collective-permute-start.7 = (bf16[128,2048]{1,0:T(8,128)(2,1)S(1)}, bf16[128,2048]{1,0:T(8,128)(2,1)S(1)}, u32[]{:S(2)}, u32[]{:S(2)}) collective-permute-start(bf16[128,2048]{1,0:T(8,128)(2,1)S(1)} %pad_maximum_fusion.1), channel_id=1, source_target_pairs={{0,6},{1,7},{2,0},{3,1},{4,2},{5,3},{6,4},{7,5},{8,14},{9,15},{10,... | collective-permute-start | bytes 1572872 | tf_op jit(solution)/shard_map/ppermute | solution.py:40
  76.1 7.3 %collective-permute-done.10 = bf16[128,2048]{1,0:T(8,128)(2,1)S(1)} collective-permute-done((bf16[128,2048]{1,0:T(8,128)(2,1)S(1)}, bf16[128,2048]{1,0:T(8,128)(2,1)S(1)}, u32[]{:S(2)}, u32[]{:S(2)}) %collective-permute-start.10) | collective-permute-done | bytes 524320 | tf_op jit(solution)/shard_map/ppermute | solution.py:40
  83.8 2.1 collective-permute-done.6
  86.3 4.7 %collective-permute-done.12 = bf16[2,32,2048]{2,1,0:T(8,128)(2,1)S(1)} collective-permute-done((bf16[2,32,2048]{2,1,0:T(8,128)(2,1)S(1)}, bf16[2,32,2048]{2,1,0:T(8,128)(2,1)S(1)}, u32[]{:S(2)}, u32[]{:S(2)}) %collective-permute-start.12) | collective-permute-done | bytes 262176 | tf_op jit(solution)/shard_map/ppermute | solution.py:40
  92.5 3.6 %collective-permute-done.13 = bf16[32,2048]{1,0:T(8,128)(2,1)S(1)} collective-permute-done((bf16[32,2048]{1,0:T(8,128)(2,1)S(1)}, bf16[32,2048]{1,0:T(8,128)(2,1)S(1)}, u32[]{:S(2)}, u32[]{:S(2)}) %collective-permute-start.13) | collective-permute-done | bytes 131104 | tf_op jit(solution)/shard_map/ppermute | solution.py:40
  97.2 2.0 dispatch.1
  99.2 65.8 %all_to_all.15 = bf16[128,16,1024]{2,1,0:T(8,128)(2,1)S(1)} all-to-all(bf16[128,16,1024]{2,1,0:T(8,128)(2,1)S(1)} %bitcast.39), channel_id=1, replica_groups=mesh['prompt'=4,'sample'=32] {'sample','prompt'}, dimensions={0} | all-to-all | bytes 8388608 | tf_op jit(solution)/shard_map/all_to_all | solution.py:533
  165.0 15.6 %expert.1 = bf16[2048,1024]{1,0:T(8,128)(2,1)S(1)} custom-call(bf16[2048,1024]{1,0:T(8,128)(2,1)S(1)} %bitcast.40, bf16[4096,1536]{1,0:T(8,128)(2,1)} %bitcast.49, bf16[768,4096]{1,0:T(8,128)(2,1)} %bitcast.50), custom_call_target="tpu_custom_call" | custom-call | flops 9663676416 | bytes 28311552 | tf_op jit(solution)/shard_map/expert/pallas_call | solution.py:459
  180.7 57.1 %all_to_all.16 = bf16[128,16,1024]{2,1,0:T(8,128)(2,1)S(1)} all-to-all(bf16[128,16,1024]{2,1,0:T(8,128)(2,1)S(1)} %bitcast.41), channel_id=1, replica_groups=mesh['prompt'=4,'sample'=32] {'sample','prompt'}, dimensions={0} | all-to-all | bytes 8388608 | tf_op jit(solution)/shard_map/all_to_all | solution.py:537
  237.7 2.5 %combine.1 = bf16[2,16,4096]{2,1,0:T(8,128)(2,1)} custom-call(bf16[256,2048]{1,0:T(8,128)(2,1)S(1)} %get-tuple-element.30.map_ref, bf16[2048,1024]{1,0:T(8,128)(2,1)S(1)} %bitcast.38, f32[128,1024]{1,0:T(8,128)S(1)} %get-tuple-element.32.hidden_ref), custom_call_target="tpu_custom_call" | custom-call | flops 1073741824 | bytes 6291456 | tf_op jit(solution)/shard_map/combine/pallas_call | solution.py:379
  (78 shorter events, 6.7 us)
Async XLA Ops:
  0.0 40.3 %copy-start.6 = (s32[2,16,8]{1,2,0:T(8,128)S(1)}, s32[2,16,8]{1,2,0:T(8,128)}, u32[]{:S(2)}) copy-start(s32[2,16,8]{1,2,0:T(8,128)} %param.18) | copy-start | bytes 3076
  2.6 32.4 %all-to-all-start = ((bf16[16,112,512]{2,1,0:T(8,128)(2,1)}), bf16[16,112,512]{2,1,0:T(8,128)(2,1)S(1)}, u32[]{:S(2)}, u32[]{:S(2)}) async-start(bf16[16,112,512]{2,1,0:T(8,128)(2,1)} %pack.1), calls=%async_computation | async-start | bytes 3670016 | tf_op jit(solution)/shard_map/all_to_all | solution.py:512
  11.2 38.4 %collective-permute-start = (bf16[256,4096]{1,0:T(8,128)(2,1)}, bf16[256,4096]{1,0:T(8,128)(2,1)}, u32[]{:S(2)}, u32[]{:S(2)}) collective-permute-start(bf16[256,4096]{1,0:T(8,128)(2,1)} %own_ref.3), channel_id=1, source_target_pairs={{0,1},{1,0},{2,3},{3,2},{4,5},{5,4},{6,7},{7,6},{8,9},{9,8},{10,11... | collective-permute-start | bytes 6291464 | tf_op jit(solution)/shard_map/ppermute | solution.py:40
  36.2 6.7 %collective-permute-start.1 = (bf16[16,64,512]{2,1,0:T(8,128)(2,1)}, bf16[16,64,512]{2,1,0:T(8,128)(2,1)S(1)}, u32[]{:S(2)}, u32[]{:S(2)}) collective-permute-start(bf16[16,64,512]{2,1,0:T(8,128)(2,1)} %slice.62), channel_id=1, source_target_pairs={{0,1},{1,0},{2,3},{3,2},{4,5},{5,4},{6,7},{7,6},{8,9},{9,8},{10,11... | collective-permute-start | bytes 3145736 | tf_op jit(solution)/shard_map/ppermute | solution.py:40
  41.5 8.2 %copy-start = (bf16[256,4096]{1,0:T(8,128)(2,1)S(1)}, bf16[256,4096]{1,0:T(8,128)(2,1)}, u32[]{:S(2)}) copy-start(bf16[256,4096]{1,0:T(8,128)(2,1)} %own_ref.3) | copy-start | bytes 6291460
  42.8 9.9 %copy-start.2 = (bf16[16,64,512]{2,1,0:T(8,128)(2,1)}, bf16[16,64,512]{2,1,0:T(8,128)(2,1)S(1)}, u32[]{:S(2)}) copy-start(bf16[16,64,512]{2,1,0:T(8,128)(2,1)S(1)} %collective-permute-done.1.other_hbm) | copy-start | bytes 3145732
  49.6 8.4 %copy-start.7 = (f32[2,16,8]{1,2,0:T(8,128)S(1)}, f32[2,16,8]{1,2,0:T(8,128)}, u32[]{:S(2)}) copy-start(f32[2,16,8]{1,2,0:T(8,128)} %param.19) | copy-start | bytes 3076
  52.7 13.7 %collective-permute-start.2 = (bf16[64,2048]{1,0:T(8,128)(2,1)}, bf16[64,2048]{1,0:T(8,128)(2,1)S(1)}, u32[]{:S(2)}, u32[]{:S(2)}) collective-permute-start(bf16[64,2048]{1,0:T(8,128)(2,1)} %get-tuple-element.20), channel_id=1, source_target_pairs={{0,2},{1,3},{2,4},{3,5},{4,6},{5,7},{6,0},{7,1},{8,10},{9,11},{10,... | collective-permute-start | bytes 786440 | tf_op jit(solution)/shard_map/ppermute | solution.py:40
  52.7 13.7 %collective-permute-start.3 = (bf16[64,2048]{1,0:T(8,128)(2,1)}, bf16[64,2048]{1,0:T(8,128)(2,1)S(1)}, u32[]{:S(2)}, u32[]{:S(2)}) collective-permute-start(bf16[64,2048]{1,0:T(8,128)(2,1)} %get-tuple-element.21), channel_id=1, source_target_pairs={{0,6},{1,7},{2,0},{3,1},{4,2},{5,3},{6,4},{7,5},{8,14},{9,15},{10,... | collective-permute-start | bytes 786440 | tf_op jit(solution)/shard_map/ppermute | solution.py:40
  55.4 11.1 %collective-permute-start.4 = (bf16[64,2048]{1,0:T(8,128)(2,1)}, bf16[64,2048]{1,0:T(8,128)(2,1)S(1)}, u32[]{:S(2)}, u32[]{:S(2)}) collective-permute-start(bf16[64,2048]{1,0:T(8,128)(2,1)} %get-tuple-element.22), channel_id=1, source_target_pairs={{0,8},{1,9},{2,10},{3,11},{4,12},{5,13},{6,14},{7,15},{8,16},{9,17... | collective-permute-start | bytes 786440 | tf_op jit(solution)/shard_map/ppermute | solution.py:40
  55.7 10.8 %collective-permute-start.5 = (bf16[64,2048]{1,0:T(8,128)(2,1)S(1)}, bf16[64,2048]{1,0:T(8,128)(2,1)S(1)}, u32[]{:S(2)}, u32[]{:S(2)}) collective-permute-start(bf16[64,2048]{1,0:T(8,128)(2,1)S(1)} %get-tuple-element.23), channel_id=1, source_target_pairs={{0,24},{1,25},{2,26},{3,27},{4,28},{5,29},{6,30},{7,31},{8,0},{9,1... | collective-permute-start | bytes 786440 | tf_op jit(solution)/shard_map/ppermute | solution.py:40
  58.3 8.2 %copy-start.1 = (bf16[256,4096]{1,0:T(8,128)(2,1)S(1)}, bf16[256,4096]{1,0:T(8,128)(2,1)}, u32[]{:S(2)}) copy-start(bf16[256,4096]{1,0:T(8,128)(2,1)} %own_ref.3) | copy-start | bytes 6291460
  58.3 1.4 copy-start.3
  70.2 13.2 %collective-permute-start.10 = (bf16[128,2048]{1,0:T(8,128)(2,1)S(1)}, bf16[128,2048]{1,0:T(8,128)(2,1)S(1)}, u32[]{:S(2)}, u32[]{:S(2)}) collective-permute-start(bf16[128,2048]{1,0:T(8,128)(2,1)S(1)} %pad_maximum_fusion.2), channel_id=1, source_target_pairs={{0,8},{1,9},{2,10},{3,11},{4,12},{5,13},{6,14},{7,15},{8,16},{9,17... | collective-permute-start | bytes 1572872 | tf_op jit(solution)/shard_map/ppermute | solution.py:40
  70.3 13.1 %collective-permute-start.11 = (bf16[128,2048]{1,0:T(8,128)(2,1)S(1)}, bf16[128,2048]{1,0:T(8,128)(2,1)S(1)}, u32[]{:S(2)}, u32[]{:S(2)}) collective-permute-start(bf16[128,2048]{1,0:T(8,128)(2,1)S(1)} %pad_maximum_fusion.3), channel_id=1, source_target_pairs={{0,24},{1,25},{2,26},{3,27},{4,28},{5,29},{6,30},{7,31},{8,0},{9,1... | collective-permute-start | bytes 1572872 | tf_op jit(solution)/shard_map/ppermute | solution.py:40
  73.2 12.6 %collective-permute-start.6 = (bf16[128,2048]{1,0:T(8,128)(2,1)S(1)}, bf16[128,2048]{1,0:T(8,128)(2,1)S(1)}, u32[]{:S(2)}, u32[]{:S(2)}) collective-permute-start(bf16[128,2048]{1,0:T(8,128)(2,1)S(1)} %pad_maximum_fusion), channel_id=1, source_target_pairs={{0,2},{1,3},{2,4},{3,5},{4,6},{5,7},{6,0},{7,1},{8,10},{9,11},{10,... | collective-permute-start | bytes 1572872 | tf_op jit(solution)/shard_map/ppermute | solution.py:40
  73.4 12.5 %collective-permute-start.7 = (bf16[128,2048]{1,0:T(8,128)(2,1)S(1)}, bf16[128,2048]{1,0:T(8,128)(2,1)S(1)}, u32[]{:S(2)}, u32[]{:S(2)}) collective-permute-start(bf16[128,2048]{1,0:T(8,128)(2,1)S(1)} %pad_maximum_fusion.1), channel_id=1, source_target_pairs={{0,6},{1,7},{2,0},{3,1},{4,2},{5,3},{6,4},{7,5},{8,14},{9,15},{10,... | collective-permute-start | bytes 1572872 | tf_op jit(solution)/shard_map/ppermute | solution.py:40
  83.6 13.6 %copy-start.4 = (bf16[2,16,4096]{2,1,0:T(8,128)(2,1)S(1)}, bf16[2,16,4096]{2,1,0:T(8,128)(2,1)}, u32[]{:S(2)}) copy-start(bf16[2,16,4096]{2,1,0:T(8,128)(2,1)} %residual_ref.1) | copy-start | bytes 786436
  83.6 13.6 %copy-start.5 = (f32[4096]{0:T(1024)S(1)}, f32[4096]{0:T(1024)}, u32[]{:S(2)}) copy-start(f32[4096]{0:T(1024)} %param.15) | copy-start | bytes 49156
  83.7 7.3 %collective-permute-start.12 = (bf16[2,32,2048]{2,1,0:T(8,128)(2,1)S(1)}, bf16[2,32,2048]{2,1,0:T(8,128)(2,1)S(1)}, u32[]{:S(2)}, u32[]{:S(2)}) collective-permute-start(bf16[2,32,2048]{2,1,0:T(8,128)(2,1)S(1)} %pad_maximum_fusion.5), channel_id=1, source_target_pairs={{0,2},{1,3},{2,0},{3,1},{4,6},{5,7},{6,4},{7,5},{8,10},{9,11},{10,... | collective-permute-start | bytes 786440 | tf_op jit(solution)/shard_map/ppermute | solution.py:40
  86.2 5.6 %collective-permute-start.8 = (bf16[2,32,2048]{2,1,0:T(8,128)(2,1)S(1)}, bf16[2,32,2048]{2,1,0:T(8,128)(2,1)S(1)}, u32[]{:S(2)}, u32[]{:S(2)}) collective-permute-start(bf16[2,32,2048]{2,1,0:T(8,128)(2,1)S(1)} %pad_maximum_fusion.4), channel_id=1, source_target_pairs={{0,8},{1,9},{2,10},{3,11},{4,12},{5,13},{6,14},{7,15},{8,0},{9,1},... | collective-permute-start | bytes 786440 | tf_op jit(solution)/shard_map/ppermute | solution.py:40
  91.0 5.1 %collective-permute-start.13 = (bf16[32,2048]{1,0:T(8,128)(2,1)S(1)}, bf16[32,2048]{1,0:T(8,128)(2,1)S(1)}, u32[]{:S(2)}, u32[]{:S(2)}) collective-permute-start(bf16[32,2048]{1,0:T(8,128)(2,1)S(1)} %fusion.3), channel_id=1, source_target_pairs={{0,6},{1,7},{2,4},{3,5},{4,2},{5,3},{6,0},{7,1},{8,14},{9,15},{10,... | collective-permute-start | bytes 393224 | tf_op jit(solution)/shard_map/ppermute | solution.py:40
  91.8 5.3 %collective-permute-start.9 = (bf16[32,2048]{1,0:T(8,128)(2,1)S(1)}, bf16[32,2048]{1,0:T(8,128)(2,1)S(1)}, u32[]{:S(2)}, u32[]{:S(2)}) collective-permute-start(bf16[32,2048]{1,0:T(8,128)(2,1)S(1)} %fusion.2), channel_id=1, source_target_pairs={{0,24},{1,25},{2,26},{3,27},{4,28},{5,29},{6,30},{7,31},{8,16},{9,... | collective-permute-start | bytes 393224 | tf_op jit(solution)/shard_map/ppermute | solution.py:40
